TPU v7x, 512 devices: a whole 4x8x8 slice. The times are simulated.
512 devices in a mesh: season: 16 (over z, core), farm: 32 (over x, y).
Axes of the slice: x: 4, y: 8, z: 8, core: 2. Of those that a mesh axis runs over, the one named last changes fastest.
Arguments:
- station_index: bfloat16 [32768, 10240], P('farm', 'season'), may hold values from -6 to 6
- strike_day: int32 [32768], P('farm'), may hold values from 0 to 63
- exit_day: int32 [32768], P('farm'), may hold values from 65 to 128
- farm_yield: bfloat16 [32768, 10240], P('farm', 'season'), as said below
- send_list: int32 [32, 32, 2], P('farm'), may hold values from 0 to 7, as said below
- pair_list: int32 [2048, 2], P('farm'), may hold values from 0 to 255, as said below
Outputs:
- gram: float32 [128, 2048, 128], P('season', 'farm')
Inputs may be any that keep to these rules, and one draw needn't show every extreme that they name: `send_list`: each entry names a local station block of the source farm index; the 2 entries of one source and destination are distinct. `pair_list`: the rows of farm index d name, in the first column, farm blocks d * 8 to d * 8 + 7, and in the second a slot s = q * 2 + c whose place c is below the number of blocks source q relays to d; a farm index relays 2 blocks to itself, and 1 to 2 to each other one. `farm_yield`: finite yield proxies with a level and a drift over the days.
All inputs are finite; a program needn't handle non-finite values.
Results may differ from a plain program's by a relative error of at most 0.0032.
Values may be sent and summed in bfloat16 or wider, within the bound.
No kernel may reach another device: no remote copies, remote signals or barrier semaphores. Data moves between devices by JAX's collectives and lax.ppermute only.
A program may use at most 128 MiB of HBM per device.

v0:
```python
import jax
import jax.numpy as jnp
from jax import lax
from jax.sharding import PartitionSpec as P

SEASON_DAYS = 128
FBLOCK = 128
SBLOCK = 128
FB_DEV = 8


def payout(series, strike_days, exit_days):
    row_total, day_total = series.shape
    shaped = series.reshape(row_total, day_total // SEASON_DAYS, SEASON_DAYS)
    day_index = lax.broadcasted_iota(jnp.int32, (1, 1, SEASON_DAYS), 2).astype(jnp.float32)
    start_on = day_index >= strike_days.astype(jnp.float32)[:, None, None]
    masked = jnp.where(start_on, shaped, jnp.zeros_like(shaped))
    upper_mask = (
        lax.broadcasted_iota(jnp.int32, (SEASON_DAYS, SEASON_DAYS), 0)
        <= lax.broadcasted_iota(jnp.int32, (SEASON_DAYS, SEASON_DAYS), 1)
    ).astype(jnp.bfloat16)
    running = jnp.einsum("rsu,ut->rst", masked, upper_mask, preferred_element_type=jnp.float32)
    window_on = start_on & (day_index < exit_days.astype(jnp.float32)[:, None, None])
    value = jax.nn.softplus(0.3 * running + shaped.astype(jnp.float32))
    result = jnp.where(window_on, value, jnp.zeros_like(value))
    return result.astype(jnp.bfloat16).reshape(row_total, day_total)


def shards(station_index, strike_day, exit_day, farm_yield, send_list, pair_list):
    farm_rows, day_total = farm_yield.shape
    season_count = lax.axis_size("season")
    all_days = day_total * season_count
    values_f = farm_yield.astype(jnp.float32)
    totals = lax.psum(jnp.sum(values_f, axis=1), "season")
    center = totals / all_days
    offset = values_f - center[:, None]
    spread = lax.psum(jnp.sum(offset * offset, axis=1), "season") / all_days
    scaled = (offset * lax.rsqrt(spread + 1e-05)[:, None]).astype(jnp.bfloat16)
    local_list = send_list[0]
    block_total = station_index.shape[0] // SBLOCK
    paid = payout(station_index, strike_day, exit_day)
    outgoing = paid.reshape(block_total, SBLOCK, day_total)[local_list]
    arrived = lax.all_to_all(outgoing, "farm", split_axis=0, concat_axis=0, tiled=True)
    slot_rows = arrived.reshape(-1, SBLOCK, day_total)
    farm_local = pair_list[:, 0] - lax.axis_index("farm") * FB_DEV
    chosen = slot_rows[pair_list[:, 1]]
    farm_blocks = scaled.reshape(farm_rows // FBLOCK, FBLOCK, day_total)[farm_local]
    factor = float(all_days) ** (-0.5)
    product = jnp.einsum("pcd,psd->cps", farm_blocks, chosen, preferred_element_type=jnp.float32)
    return lax.psum_scatter(product * factor, "season", scatter_dimension=0, tiled=True)


def solution(mesh):
    return jax.shard_map(
        shards,
        mesh=mesh,
        in_specs=(
            P("farm", "season"),
            P("farm"),
            P("farm"),
            P("farm", "season"),
            P("farm", None, None),
            P("farm", None),
        ),
        out_specs=P("season", "farm", None),
        check_vma=False,
    )
```

profile of v0, /device:TPU:6, one launch (start us, length us, event | category | flops | bytes accessed | tf_op | source)
XLA Modules:
  0.0 382.5 jit_solution(3794827851830684919)
XLA Ops:
  6.5 0.7 compare_select_fusion.1
  7.2 0.7 convert_element_type.30
  7.9 0.7 convert_element_type.31
  8.7 0.1 reshape.128
  8.8 0.3 compare_and_fusion
  9.2 0.2 copy.24
  9.4 1.6 copy.25
  11.0 0.8 copy.27
  11.8 2.2 fusion.5
  14.0 0.9 copy.33
  14.9 1.6 reshape.152
  16.5 6.6 %gather_fusion = bf16[64,128,640]{2,1,0:T(8,128)(2,1)} fusion(bf16[8,128,640]{2,1,0:T(8,128)(2,1)S(1)} %reshape.152, s32[1024]{0:T(1024)S(1)} %pad_clamp_fusion.2), kind=kCustom, calls=%fused_computation | custom fusion | bytes 20971776 | tf_op jit(solution)/shard_map/gather | solution.py:42
  23.2 10.8 %all-to-all-start = ((bf16[32,2,128,640]{3,2,1,0:T(8,128)(2,1)}), bf16[32,2,128,640]{3,2,1,0:T(8,128)(2,1)}, u32[]{:S(2)}, u32[]{:S(2)}) async-start(bf16[32,2,128,640]{3,2,1,0:T(8,128)(2,1)} %bitcast.20), calls=%async_computation | async-start | bytes 20971520 | tf_op jit(solution)/shard_map/all_to_all | solution.py:43
  34.1 0.2 convert_reduce_fusion
  34.3 32.7 %psum.14 = f32[1024]{0:T(1024)S(1)} all-reduce(f32[1024]{0:T(1024)S(1)} %convert_reduce_fusion), channel_id=1, replica_groups=mesh['season'=16,'farm'=32] {'season'}, use_global_device_ids=true, to_apply=%region_1.0 | all-reduce | flops 1024 | bytes 8192 | tf_op jit(solution)/shard_map/psum | solution.py:34
  67.0 0.5 fusion.2
  67.6 25.3 %psum.15 = f32[1024]{0:T(1024)S(1)} all-reduce(f32[1024]{0:T(1024)S(1)} %fusion.2), channel_id=1, replica_groups=mesh['season'=16,'farm'=32] {'season'}, use_global_device_ids=true, to_apply=%region_3.0 | all-reduce | flops 1024 | bytes 8192 | tf_op jit(solution)/shard_map/psum | solution.py:37
  92.9 0.4 fusion.3
  93.4 6.7 %gather_fusion.2 = bf16[64,128,640]{2,1,0:T(8,128)(2,1)} fusion(bf16[8,128,640]{2,1,0:T(8,128)(2,1)S(1)} %bitcast.19, s32[1024]{0:T(1024)S(1)} %get-tuple-element.9), kind=kCustom, calls=%fused_computation.2 | custom fusion | bytes 20971776 | tf_op jit(solution)/shard_map/gather | solution.py:47
  100.0 165.6 %all-to-all-done = bf16[32,2,128,640]{3,2,1,0:T(8,128)(2,1)} async-done(((bf16[32,2,128,640]{3,2,1,0:T(8,128)(2,1)}), bf16[32,2,128,640]{3,2,1,0:T(8,128)(2,1)}, u32[]{:S(2)}, u32[]{:S(2)}) %all-to-all-start) | async-done | bytes 10485792 | tf_op jit(solution)/shard_map/all_to_all | solution.py:43
  265.6 10.7 %gather_fusion.1 = bf16[64,128,640]{2,1,0:T(8,128)(2,1)} fusion(bf16[64,128,640]{2,1,0:T(8,128)(2,1)} %bitcast.4, s32[1024]{0:T(1024)S(1)} %get-tuple-element.10), kind=kCustom, calls=%fused_computation.1 | custom fusion | bytes 20971776 | tf_op jit(solution)/shard_map/gather | solution.py:46
  276.3 12.7 %multiply_bitcast_fusion = f32[128,64,128]{0,2,1:T(8,128)} fusion(bf16[64,128,640]{2,1,0:T(8,128)(2,1)} %gather_fusion.1, bf16[64,128,640]{2,1,0:T(8,128)(2,1)} %gather_fusion.2), kind=kOutput, calls=%fused_computation.4 | convolution fusion | flops 1343225856 | bytes 25165824 | tf_op jit(solution)/shard_map/pcd,psd->cps/dot_general | solution.py:49
  289.0 5.4 %copy.31 = f32[128,64,128]{2,1,0:T(8,128)} copy(f32[128,64,128]{0,2,1:T(8,128)} %multiply_bitcast_fusion) | data formatting | bytes 8388608 | tf_op jit(solution)/shard_map/mul | solution.py:50
  294.4 81.2 %reduce-scatter.2.cloned.1.call-done = f32[8,64,128]{2,1,0:T(8,128)} async-done(((f32[128,64,128]{2,1,0:T(8,128)}), f32[8,64,128]{2,1,0:T(8,128)}) %reduce-scatter.2.cloned.1.call-update) | async-done | bytes 262160 | tf_op jit(solution)/shard_map/reduce_scatter | solution.py:50
  (13 shorter events, 0.2 us)
Async XLA Ops:
  23.2 10.9 %copy-start = (bf16[1024,640]{1,0:T(8,128)(2,1)S(1)}, bf16[1024,640]{1,0:T(8,128)(2,1)}, u32[]{:S(2)}) copy-start(bf16[1024,640]{1,0:T(8,128)(2,1)} %param.9) | copy-start | bytes 3932164
  23.2 242.4 %all-to-all-start = ((bf16[32,2,128,640]{3,2,1,0:T(8,128)(2,1)}), bf16[32,2,128,640]{3,2,1,0:T(8,128)(2,1)}, u32[]{:S(2)}, u32[]{:S(2)}) async-start(bf16[32,2,128,640]{3,2,1,0:T(8,128)(2,1)} %bitcast.20), calls=%async_computation | async-start | bytes 20971520 | tf_op jit(solution)/shard_map/all_to_all | solution.py:43
  34.0 58.9 %copy-start.1 = (s32[64,2]{0,1:T(2,128)S(1)}, s32[64,2]{0,1:T(2,128)}, u32[]{:S(2)}) copy-start(s32[64,2]{0,1:T(2,128)} %param.11) | copy-start | bytes 1540
  34.0 341.7 %reduce-scatter.2.cloned.1.call-start = ((), (), s32[]{:S(2)}) async-start(), calls=%async_computation.2 | async-start | bytes 4456448 | tf_op jit(solution)/shard_map/reduce_scatter | solution.py:50
Sparse Core Ops, SparseCore 0:
  294.5 81.0 reduce-scatter.1
where the time goes:
time: 383 us
  waiting for transfers between devices  247 us (64%)
  blocking collectives  58 us (15%)
  local copies, waits for them, and re-layouts  34.8 us (9%)
  matrix products  14.8 us (4%)
  between operations  13.5 us (4%)
  starting transfers between devices  10.9 us (3%)
    all_to_all x1, waiting for transfers between devices, shards(): lax.all_to_all(outgoing, 'farm', split_axis=0, concat_axis=0, tiled=True)  166 us
    reduce_scatter x1, waiting for transfers between devices, shards(): lax.psum_scatter(product * factor, 'season', scatter_dimension=0, tiled=T...  81.2 us
    psum x1, blocking collectives, shards(): totals = lax.psum(jnp.sum(values_f, axis=1), 'season')  32.7 us
    psum x1, blocking collectives, shards(): spread = lax.psum(jnp.sum(offset * offset, axis=1), 'season') / all_days  25.3 us
    dot_general x1, matrix products, shards(): jnp.einsum('pcd,psd->cps', farm_blocks, chosen, preferred_element_type=jn...  12.7 us
    all_to_all x1, starting transfers between devices, shards(): lax.all_to_all(outgoing, 'farm', split_axis=0, concat_axis=0, tiled=True)  10.8 us
    gather x1, local copies, waits for them, and re-layouts, shards(): chosen = slot_rows[pair_list[:, 1]]  10.7 us
  transfers between devices with their start and end apart: 2, of which 2 were waited for; matrix products, arithmetic and copies ran while one was open for 2% of the time, Pallas kernels for 0%

commit v1 on v0

v1 whole, which is shorter than its diff:
```python
import jax
import jax.numpy as jnp
from jax import lax
from jax.experimental import pallas as pl
from jax.experimental.pallas import tpu as pltpu
from jax.sharding import PartitionSpec as P

DAY = 128
BLK = 128
NX, NY, NZ = 4, 8, 8
FB_DEV = 8
GATE = 2
STEPS = (2, 1, 3)
VMEM_CAP = 48 * 1024 * 1024


def y_shift(k):
    return [(x * NY + y, x * NY + (y + k) % NY) for x in range(NX) for y in range(NY)]


ROWS = [[x * NY + y for y in range(NY)] for x in range(NX)]


def x_shift(k):
    return [(x * NY + y, ((x + k) % NX) * NY + y) for x in range(NX) for y in range(NY)]


def z_shift(k):
    return [(z * 2 + c, ((z + k) % NZ) * 2 + c) for z in range(NZ) for c in range(2)]


CORE_SWAP = [(i, i ^ 1) for i in range(2 * NZ)]


def payout_kernel(first, strike_ref, exit_ref, series_ref, out_ref):
    b = pl.program_id(0) + first
    tau = lax.broadcasted_iota(jnp.int32, (BLK, DAY), 1)
    row = lax.broadcasted_iota(jnp.int32, (BLK, DAY), 0)
    upper = jnp.where(row <= tau, 1.0, 0.0).astype(jnp.bfloat16)
    tau = tau.astype(jnp.float32)

    def column(ref):
        line = ref[pl.ds(b, 1), :].astype(jnp.float32)
        return jnp.transpose(jnp.broadcast_to(line, (BLK, BLK)))

    start_on = tau >= column(strike_ref)
    window_on = start_on & (tau < column(exit_ref))
    for s in range(out_ref.shape[2] // DAY):
        days = slice(s * DAY, (s + 1) * DAY)
        x = series_ref[:, days].astype(jnp.float32)
        masked = jnp.where(start_on, x, 0.0).astype(jnp.bfloat16)
        running = jnp.dot(masked, upper, preferred_element_type=jnp.float32)
        v = 0.3 * running + x
        value = jnp.maximum(v, 0.0) + jnp.log1p(jnp.exp(-jnp.abs(v)))
        out_ref[0, :, days] = jnp.where(window_on, value, 0.0).astype(jnp.bfloat16)


def payouts(series, strike, leave, first, count, before=None, gate=None):
    rows, days = series.shape
    blocks = rows // BLK
    lines = pl.BlockSpec((blocks, BLK), lambda b: (0, 0))
    operands = [strike.reshape(blocks, BLK), leave.reshape(blocks, BLK), series]
    specs = [lines, lines, pl.BlockSpec((BLK, days), lambda b: (b + first, 0))]
    alias = {}
    if before is not None:
        operands += [before, gate]
        specs += [pl.BlockSpec(memory_space=pl.ANY)] * 2
        alias = {3: 0}
    return pl.pallas_call(
        lambda *refs: payout_kernel(first, *refs[:3], refs[-1]),
        grid=(count,),
        out_shape=jax.ShapeDtypeStruct((blocks, BLK, days), jnp.bfloat16),
        in_specs=specs,
        out_specs=pl.BlockSpec((1, BLK, days), lambda b: (b + first, 0, 0)),
        input_output_aliases=alias,
        name="payouts",
    )(*operands)


def pick_kernel(backs, table_ref, place_ref, *refs):
    outs, held, sems = refs[-2 - len(STEPS):-2], refs[-2], refs[-1]
    half = BLK // 2
    copies = []
    for step, out in zip(STEPS, outs):
        x = lax.rem(place_ref[0] + step, NX)
        for i, back in enumerate(backs):
            line = 0 if back is None else lax.rem(place_ref[1] + NY - back, NY)
            for c in range(2):
                block = table_ref[line, x * 2 + c]
                n, where = len(copies), out.at[2 * i + c]
                if refs[0].shape[1] == BLK:
                    copies.append((refs[i].at[block], where, n, 0, BLK))
                else:
                    for h in range(2):
                        copies.append((refs[h].at[block], where.at[pl.ds(h * half, half)], n, h * half, half))
    inward, outward = [], []
    for n, (src, dst, at, low, rows) in enumerate(copies):
        copy = pltpu.make_async_copy(src, held.at[at, pl.ds(low, rows)], sems.at[0, n])
        copy.start()
        inward.append(copy)
    for n, (src, dst, at, low, rows) in enumerate(copies):
        inward[n].wait()
        copy = pltpu.make_async_copy(held.at[at, pl.ds(low, rows)], dst, sems.at[1, n])
        copy.start()
        outward.append(copy)
    for copy in outward:
        copy.wait()


def picks(table, place, sources, backs, gate=()):
    days = sources[0].shape[-1]
    count = 2 * len(backs)
    number = count * len(STEPS) * (1 if sources[0].shape[1] == BLK else 2)
    operands = list(sources) + list(gate)
    return pl.pallas_call(
        lambda *refs: pick_kernel(backs, *refs),
        out_shape=[jax.ShapeDtypeStruct((count, BLK, days), jnp.bfloat16)] * len(STEPS),
        in_specs=[pl.BlockSpec(memory_space=pltpu.SMEM)] * 2 + [pl.BlockSpec(memory_space=pl.ANY)] * len(operands),
        out_specs=[pl.BlockSpec(memory_space=pl.ANY)] * len(STEPS),
        scratch_shapes=[pltpu.VMEM((number, BLK, days), jnp.bfloat16), pltpu.SemaphoreType.DMA((2, number))],
        compiler_params=pltpu.CompilerParams(vmem_limit_bytes=VMEM_CAP),
        cost_estimate=pl.CostEstimate(flops=0, bytes_accessed=number * BLK * days * 4, transcendentals=0),
        name="picks",
    )(table, place, *operands)


def gram_kernel(factor, table_ref, place_ref, pair_ref, farm_ref, *refs):
    held, relayed = refs[:9], refs[9:24]
    keep_ref, send_ref, slots, sems = refs[24:]
    x, y, z, core = place_ref[0], place_ref[1], place_ref[2], place_ref[3]
    copies = []
    half = BLK // 2
    for at, back in enumerate((0, 1, 7, 2, 6, 3, 5, 4)):
        for c in range(2):
            block = table_ref[lax.rem(y + NY - back, NY), x * 2 + c]
            if at < 7:
                copies.append((held[at].at[block], slots.at[0, 2 * at + c]))
            else:
                for h in range(2):
                    copies.append((held[7 + h].at[block], slots.at[0, 2 * at + c, pl.ds(h * half, half)]))
    for i, step in enumerate(STEPS):
        at = 0
        for ref in relayed[i::len(STEPS)]:
            n = ref.shape[0]
            copies.append((ref, slots.at[step, pl.ds(at, n)]))
            at += n
    started = []
    for n, (src, dst) in enumerate(copies):
        copy = pltpu.make_async_copy(src, dst, sems.at[n])
        copy.start()
        started.append(copy)
    for copy in started:
        copy.wait()

    first = (x * NY + y) * FB_DEV

    def one(p):
        farm = pair_ref[p, 0] - first
        slot = pair_ref[p, 1]
        source, c = slot // 2, lax.rem(slot, 2)
        sx, sy = source // NY, lax.rem(source, NY)
        dy = lax.rem(y - sy + NY, NY)
        place = jnp.where(dy == 0, 0, jnp.where(dy < 4, 2 * dy - 1, jnp.where(dy == 4, 7, 2 * (NY - dy))))
        product = lax.dot_general(
            farm_ref[farm], slots[lax.rem(x - sx + NX, NX), place * 2 + c], (((1,), (1,)), ((), ())), preferred_element_type=jnp.float32
        ) * factor
        for target in range(NZ):
            near_rows = product[target * 16: target * 16 + 8]
            far_rows = product[target * 16 + 8: target * 16 + 16]
            d = lax.rem(target - z + NZ, NZ)
            keep_ref[d, p] = jnp.where(core == 0, near_rows, far_rows)
            send_ref[d, p] = jnp.where(core == 0, far_rows, near_rows)

    pl.loop(0, pair_ref.shape[0], unroll=4)(one)


def grams(factor, table, place, pairs, farms, stations):
    days = farms.shape[-1]
    count = pairs.shape[0]
    shape = jax.ShapeDtypeStruct((NZ, count, 8, BLK), jnp.float32)
    vmem = pl.BlockSpec(memory_space=pltpu.VMEM)
    return pl.pallas_call(
        lambda *refs: gram_kernel(factor, *refs),
        out_shape=[shape] * 2,
        in_specs=[pl.BlockSpec(memory_space=pltpu.SMEM)] * 3 + [vmem] + [pl.BlockSpec(memory_space=pl.ANY)] * len(stations),
        out_specs=[vmem] * 2,
        scratch_shapes=[pltpu.VMEM((NX, 2 * NY, BLK, days), jnp.bfloat16), pltpu.SemaphoreType.DMA((33,))],
        compiler_params=pltpu.CompilerParams(vmem_limit_bytes=VMEM_CAP),
        cost_estimate=pl.CostEstimate(flops=2 * count * BLK * BLK * days, bytes_accessed=64 * BLK * days * 2, transcendentals=0),
        name="grams",
    )(table, place, pairs, farms, *stations)


def pass_on(value, after):
    spec = pl.BlockSpec(memory_space=pl.ANY)
    return pl.pallas_call(
        lambda *refs: None,
        out_shape=jax.ShapeDtypeStruct(value.shape, value.dtype),
        in_specs=[spec] * (1 + len(after)),
        out_specs=spec,
        input_output_aliases={0: 0},
        name="pass_on",
    )(value, *after)


def standardised(farm_yield):
    rows, days = farm_yield.shape
    values = farm_yield.astype(jnp.float32)
    mean = jnp.sum(values, axis=1) / days
    offset = values - mean[:, None]
    square = jnp.sum(offset * offset, axis=1)
    state = jnp.stack([mean.reshape(-1, BLK), square.reshape(-1, BLK)])
    held = float(days)
    for hop in (CORE_SWAP, z_shift(1), z_shift(2), z_shift(4)):
        other = lax.ppermute(state, "season", hop)
        gap = other[0] - state[0]
        state = jnp.stack([
            0.5 * (state[0] + other[0]),
            state[1] + other[1] + gap * gap * (0.5 * held),
        ])
        held *= 2
    center = state[0].reshape(rows, 1)
    spread = state[1].reshape(rows, 1) / held
    scaled = ((values - center) * lax.rsqrt(spread + 1e-05)).astype(jnp.bfloat16)
    return scaled.reshape(rows // BLK, BLK, days)


def season_sum(keep, send):
    other = lax.ppermute(send, "season", CORE_SWAP)
    part = [keep[d] + other[d] for d in range(NZ)]
    half = keep.shape[1] // 2
    hop = lambda v, k: lax.ppermute(v, "season", z_shift(k))
    up4, down4 = hop(part[4][:half], 3), hop(part[4][half:], -3)
    up3, down3 = hop(part[3], 2), hop(part[5], -2)
    up2, down2 = hop(part[2], 1), hop(part[6], -1)
    right, left = part[1] + up2 + up3, part[7] + down2 + down3
    right = jnp.concatenate([right[:half] + up4, right[half:]])
    left = jnp.concatenate([left[:half], left[half:] + down4])
    total = part[0] + hop(right, 1) + hop(left, -1)
    return total.transpose(1, 0, 2)


def gates(k, relayed, farms):
    return relayed[k] if 1 <= k < 3 else []


def shards(station_index, strike_day, exit_day, farm_yield, send_list, pair_list):
    days = farm_yield.shape[1]
    all_days = days * lax.axis_size("season")
    farm, season = lax.axis_index("farm"), lax.axis_index("season")
    place = jnp.stack([farm // NY, farm % NY, season // 2, season % 2]).astype(jnp.int32)

    along = lambda v, hop: lax.ppermute(v, "farm", hop)
    wanted = send_list.reshape(NX, NY, 2).transpose(1, 0, 2)
    table = lax.all_to_all(wanted, "farm", 0, 0, axis_index_groups=ROWS, tiled=True).reshape(NY, 2 * NX)
    mine = lax.dynamic_index_in_dim(wanted, farm % NY, 0).reshape(1, 2 * NX)

    blocks = station_index.shape[0] // BLK
    start = payouts(station_index, strike_day, exit_day, 0, blocks // 2)
    own = payouts(station_index, strike_day, exit_day, blocks // 2, blocks // 2, start, table)

    farms = standardised(farm_yield)

    relayed = []

    def relay(table, sources, backs, gate=()):
        chosen = picks(table, place, sources, backs, gate)
        relayed.append([along(v, x_shift(step)) for v, step in zip(chosen, STEPS)])

    half = BLK // 2
    relay(mine, [own], (None,))
    ups, downs = [along(own, y_shift(1))], [along(own, y_shift(-1))]
    ups[0] = pass_on(ups[0], relayed[0])
    for _ in range(2):
        ups.append(along(ups[-1], y_shift(1)))
        downs.append(along(downs[-1], y_shift(-1)))
    far = [along(ups[2][:, :half], y_shift(1)), along(downs[2][:, half:], y_shift(-1))]
    for k in range(3):
        relay(table, [ups[k], downs[k]], (k + 1, NY - k - 1), gates(k, relayed, farms))
    relay(table, far, (NY // 2,), gates(3, relayed, farms))

    held = [own] + [v for k in range(3) for v in (ups[k], downs[k])] + far
    stations = held + [v for group in relayed for v in group]
    keep, send = grams(float(all_days) ** -0.5, table, place, pair_list, farms, stations)
    return season_sum(keep, send)


def solution(mesh):
    return jax.shard_map(
        shards,
        mesh=mesh,
        in_specs=(
            P("farm", "season"),
            P("farm"),
            P("farm"),
            P("farm", "season"),
            P("farm", None, None),
            P("farm", None),
        ),
        out_specs=P("season", "farm", None),
        check_vma=False,
    )
```

time: 383 us -> 272 us (0.71)
  waiting for transfers between devices: 247 us -> 74.3 us
  starting transfers between devices: 10.9 us -> 134 us
  blocking collectives: 58 us -> 0 us
  Pallas kernels: 0 us -> 43.8 us
  local copies, waits for them, and re-layouts: 34.8 us -> 9.94 us
  matrix products: 14.8 us -> 0 us
  between operations: 13.5 us -> 0.79 us
  other arithmetic: 3.65 us -> 7.54 us
    all_to_all x1, waiting for transfers between devices: 166 us -> 3.69 us  [shards(): lax.all_to_all(wanted, 'farm', 0, 0, axis_index_groups=ROWS, tiled=True)]
    ppermute x0 -> x36, starting transfers between devices: none -> 127 us  [the longest x23 72.7 us: shards(): along = lambda v, hop: lax.ppermute(v, 'farm', hop)]
    reduce_scatter x1 -> x0, waiting for transfers between devices: 81.2 us -> none  [shards(): lax.psum_scatter(product * factor, 'season', scatter_dimension=0, tiled=T...]
    ppermute x0 -> x36, waiting for transfers between devices: none -> 70.6 us  [the longest x23 44.7 us: shards(): along = lambda v, hop: lax.ppermute(v, 'farm', hop)]
    psum x2 -> x0, blocking collectives: 58 us -> none  [the longest x1 32.7 us: shards(): totals = lax.psum(jnp.sum(values_f, axis=1), 'season')]
    pallas_call x0 -> x9, Pallas kernels: none -> 43.8 us  [the longest x5 22.3 us: picks(): pl.pallas_call(lambda *refs: pick_kernel(backs, *refs), out_shape=[jax.Sh...]
    gather x3 -> x0, local copies, waits for them, and re-layouts: 24 us -> none  [the longest x1 10.7 us: shards(): chosen = slot_rows[pair_list[:, 1]]]
    dot_general x2 -> x0, matrix products: 14.8 us -> none  [the longest x1 12.7 us: shards(): jnp.einsum('pcd,psd->cps', farm_blocks, chosen, preferred_element_type=jn...]
  transfers between devices with their start and end apart: 2 -> 37, of which waited for: 2 -> 20; matrix products, arithmetic and copies ran while one was open for 2% -> 2% of each run, Pallas kernels for 0% -> 10%
where the time goes in v1:
time: 272 us; the launch traced here: 270 us
  starting transfers between devices  134 us (49%)
  waiting for transfers between devices  74.3 us (27%)
  Pallas kernels  43.8 us (16%)
  local copies, waits for them, and re-layouts  9.94 us (4%)
  other arithmetic  7.54 us (3%)
    ppermute x23, starting transfers between devices, shards(): along = lambda v, hop: lax.ppermute(v, 'farm', hop)  72.7 us
    ppermute x23, waiting for transfers between devices, shards(): along = lambda v, hop: lax.ppermute(v, 'farm', hop)  44.7 us
    ppermute x8, starting transfers between devices, season_sum(): hop = lambda v, k: lax.ppermute(v, 'season', z_shift(k))  33.2 us
    pallas_call x5, Pallas kernels, picks(): pl.pallas_call(lambda *refs: pick_kernel(backs, *refs), out_shape=[jax.Sh...  22.3 us
    ppermute x8, waiting for transfers between devices, season_sum(): hop = lambda v, k: lax.ppermute(v, 'season', z_shift(k))  19.1 us
    ppermute x4, starting transfers between devices, standardised(): other = lax.ppermute(state, 'season', hop)  18.8 us
    pallas_call x1, Pallas kernels, grams(): pl.pallas_call(lambda *refs: gram_kernel(factor, *refs), out_shape=[shape...  13.4 us
    pallas_call x2, Pallas kernels, payouts(): pl.pallas_call(lambda *refs: payout_kernel(first, *refs[:3], refs[-1]), g...  8.05 us
  transfers between devices with their start and end apart: 37, of which 20 were waited for; matrix products, arithmetic and copies ran while one was open for 2% of the time, Pallas kernels for 10%

profile of v1, /device:TPU:6, one launch (start us, length us, event | category | flops | bytes accessed | tf_op | source)
XLA Modules:
  0.0 270.2 jit_solution(7242505092093842573)
XLA Ops:
  1.4 7.1 %all-to-all-start = ((s32[8,4,2]{1,2,0:T(2,128)}), s32[8,4,2]{1,2,0:T(2,128)S(1)}, u32[]{:S(2)}, u32[]{:S(2)}) async-start(s32[8,4,2]{1,2,0:T(2,128)} %copy.29), calls=%async_computation | async-start | bytes 16384 | tf_op jit(solution)/shard_map/all_to_all | solution.py:255
  8.6 4.0 %payouts.2.refs_3_ = bf16[8,128,640]{2,1,0:T(8,128)(2,1)} custom-call(s32[8,128]{1,0:T(8,128)} %bitcast.137, s32[8,128]{1,0:T(8,128)} %bitcast.139, bf16[1024,640]{1,0:T(8,128)(2,1)} %refs_2_.4), custom_call_target="tpu_custom_call" | custom-call | tf_op jit(solution)/shard_map/payouts/pallas_call | solution.py:69
  17.0 4.0 %payouts.3.refs_2_.refs_4_ = bf16[8,128,640]{2,1,0:T(8,128)(2,1)} custom-call(s32[8,128]{1,0:T(8,128)} %bitcast.138, s32[8,128]{1,0:T(8,128)} %bitcast.140, bf16[1024,640]{1,0:T(8,128)(2,1)} %refs_2_.4, bf16[8,128,640]{2,1,0:T(8,128)(2,1)} %payouts.2.refs_3_, s32[8,8]{1,0:T(8,128)} %copy.37.refs_4_.refs_0_), custom_call_target="tpu_custom_call", output_to_operand_aliasing={{}: (3, {})} | custom-call | tf_op jit(solution)/shard_map/payouts/pallas_call | solution.py:69
  35.2 4.0 %collective-permute-start.6 = (bf16[2,128,640]{2,1,0:T(8,128)(2,1)S(1)}, bf16[2,128,640]{2,1,0:T(8,128)(2,1)S(1)}, u32[]{:S(2)}, u32[]{:S(2)}) collective-permute-start(bf16[2,128,640]{2,1,0:T(8,128)(2,1)S(1)} %get-tuple-element.23), channel_id=1, source_target_pairs={{0,8},{1,9},{2,10},{3,11},{4,12},{5,13},{6,14},{7,15},{8,16},{9,17... | collective-permute-start | bytes 983048 | tf_op jit(solution)/shard_map/ppermute | solution.py:253
  41.1 11.1 %collective-permute-done.8.refs_3_.refs_6_ = bf16[8,128,640]{2,1,0:T(8,128)(2,1)S(1)} collective-permute-done((bf16[8,128,640]{2,1,0:T(8,128)(2,1)}, bf16[8,128,640]{2,1,0:T(8,128)(2,1)S(1)}, u32[]{:S(2)}, u32[]{:S(2)}) %collective-permute-start.8) | collective-permute-done | bytes 1310752 | tf_op jit(solution)/shard_map/ppermute | solution.py:253
  61.3 6.5 %picks.6 = (bf16[4,128,640]{2,1,0:T(8,128)(2,1)S(1)}, bf16[4,128,640]{2,1,0:T(8,128)(2,1)S(1)}, bf16[4,128,640]{2,1,0:T(8,128)(2,1)S(1)}) custom-call(s32[8,8]{1,0:T(8,128)S(1)} %copy-done.18, s32[4]{0:T(128)S(1)} %pad_add_fusion.refs_1_, bf16[8,128,640]{2,1,0:T(8,128)(2,1)S(1)} %copy-done.2, bf16[8,128,640]{2,1,0:T(8,128)(2,1)S(1)} %collective-permute-done.8.refs_3_.refs_6_), custom_call_target="tpu_custom_call" | custom-call | bytes 3932160 | tf_op jit(solution)/shard_map/picks/pallas_call | solution.py:115
  72.2 4.0 %collective-permute-start.16 = (bf16[4,128,640]{2,1,0:T(8,128)(2,1)S(1)}, bf16[4,128,640]{2,1,0:T(8,128)(2,1)S(1)}, u32[]{:S(2)}, u32[]{:S(2)}) collective-permute-start(bf16[4,128,640]{2,1,0:T(8,128)(2,1)S(1)} %get-tuple-element.26), channel_id=1, source_target_pairs={{0,8},{1,9},{2,10},{3,11},{4,12},{5,13},{6,14},{7,15},{8,16},{9,17... | collective-permute-start | bytes 1966088 | tf_op jit(solution)/shard_map/ppermute | solution.py:253
  78.1 4.3 %collective-permute-done.10.refs_3_.refs_8_ = bf16[8,128,640]{2,1,0:T(8,128)(2,1)} collective-permute-done((bf16[8,128,640]{2,1,0:T(8,128)(2,1)S(1)}, bf16[8,128,640]{2,1,0:T(8,128)(2,1)}, u32[]{:S(2)}, u32[]{:S(2)}) %collective-permute-start.10) | collective-permute-done | bytes 1310752 | tf_op jit(solution)/shard_map/ppermute | solution.py:253
  82.5 5.4 %collective-permute-start.12 = (bf16[8,128,640]{2,1,0:T(8,128)(2,1)}, bf16[8,128,640]{2,1,0:T(8,128)(2,1)S(1)}, u32[]{:S(2)}, u32[]{:S(2)}) collective-permute-start(bf16[8,128,640]{2,1,0:T(8,128)(2,1)} %collective-permute-done.10.refs_3_.refs_8_), channel_id=1, source_target_pairs={{0,7},{1,0},{2,1},{3,2},{4,3},{5,4},{6,5},{7,6},{8,15},{9,8},{10,9... | collective-permute-start | bytes 3932168 | tf_op jit(solution)/shard_map/ppermute | solution.py:253
  100.5 5.2 %picks.7 = (bf16[4,128,640]{2,1,0:T(8,128)(2,1)S(1)}, bf16[4,128,640]{2,1,0:T(8,128)(2,1)S(1)}, bf16[4,128,640]{2,1,0:T(8,128)(2,1)S(1)}) custom-call(s32[8,8]{1,0:T(8,128)S(1)} %copy-done.18, s32[4]{0:T(128)S(1)} %pad_add_fusion.refs_1_, bf16[8,128,640]{2,1,0:T(8,128)(2,1)S(1)} %collective-permute-done.9.refs_2_.refs_7_, ...), custom_call_target="tpu_custom_call" | custom-call | bytes 3932160 | tf_op jit(solution)/shard_map/picks/pallas_call | solution.py:115
  115.0 4.3 %collective-permute-start.1 = (f32[2,8,128]{2,1,0:T(8,128)S(1)}, f32[2,8,128]{2,1,0:T(8,128)S(1)}, u32[]{:S(2)}, u32[]{:S(2)}) collective-permute-start(f32[2,8,128]{2,1,0:T(8,128)S(1)} %pad_maximum_fusion.3), channel_id=1, source_target_pairs={{0,64},{32,96},{64,128},{96,160},{128,192},{160,224},{192,256},{22... | collective-permute-start | bytes 24584 | tf_op jit(solution)/shard_map/ppermute | solution.py:215
  120.1 4.2 %collective-permute-start.14 = (bf16[8,64,640]{2,1,0:T(8,128)(2,1)S(1)}, bf16[8,64,640]{2,1,0:T(8,128)(2,1)S(1)}, u32[]{:S(2)}, u32[]{:S(2)}) collective-permute-start(bf16[8,64,640]{2,1,0:T(8,128)(2,1)S(1)} %slice.149), channel_id=1, source_target_pairs={{0,7},{1,0},{2,1},{3,2},{4,3},{5,4},{6,5},{7,6},{8,15},{9,8},{10,9... | collective-permute-start | bytes 1966088 | tf_op jit(solution)/shard_map/ppermute | solution.py:253
  128.8 8.6 %collective-permute-done.19.refs_5_.refs_20_ = bf16[4,128,640]{2,1,0:T(8,128)(2,1)S(1)} collective-permute-done((bf16[4,128,640]{2,1,0:T(8,128)(2,1)S(1)}, bf16[4,128,640]{2,1,0:T(8,128)(2,1)S(1)}, u32[]{:S(2)}, u32[]{:S(2)}) %collective-permute-start.19) | collective-permute-done | bytes 655392 | tf_op jit(solution)/shard_map/ppermute | solution.py:253
  139.9 4.0 %picks.8 = (bf16[4,128,640]{2,1,0:T(8,128)(2,1)}, bf16[4,128,640]{2,1,0:T(8,128)(2,1)}, bf16[4,128,640]{2,1,0:T(8,128)(2,1)}) custom-call(s32[8,8]{1,0:T(8,128)S(1)} %copy-done.18, s32[4]{0:T(128)S(1)} %pad_add_fusion.refs_1_, bf16[8,128,640]{2,1,0:T(8,128)(2,1)S(1)} %collective-permute-done.11.refs_2_.refs_9_, bf16[8,128,640]{2,1,0:T(8,128)(2,1)} %copy-done.20, ...), custom_call_target="tpu_custom_call" | custom-call | bytes 3932160 | tf_op jit(solution)/shard_map/picks/pallas_call | solution.py:115
  147.4 6.1 %collective-permute-start.2 = (f32[2,8,128]{2,1,0:T(8,128)S(1)}, f32[2,8,128]{2,1,0:T(8,128)S(1)}, u32[]{:S(2)}, u32[]{:S(2)}) collective-permute-start(f32[2,8,128]{2,1,0:T(8,128)S(1)} %pad_maximum_fusion.4), channel_id=1, source_target_pairs={{0,128},{32,160},{64,192},{96,224},{128,256},{160,288},{192,320},{... | collective-permute-start | bytes 24584 | tf_op jit(solution)/shard_map/ppermute | solution.py:215
  153.5 3.9 %collective-permute-start.22 = (bf16[4,128,640]{2,1,0:T(8,128)(2,1)}, bf16[4,128,640]{2,1,0:T(8,128)(2,1)}, u32[]{:S(2)}, u32[]{:S(2)}) collective-permute-start(bf16[4,128,640]{2,1,0:T(8,128)(2,1)} %get-tuple-element.32), channel_id=1, source_target_pairs={{0,8},{1,9},{2,10},{3,11},{4,12},{5,13},{6,14},{7,15},{8,16},{9,17... | collective-permute-start | bytes 1966088 | tf_op jit(solution)/shard_map/ppermute | solution.py:253
  162.0 6.6 %collective-permute-start.3 = (f32[2,8,128]{2,1,0:T(8,128)S(1)}, f32[2,8,128]{2,1,0:T(8,128)S(1)}, u32[]{:S(2)}, u32[]{:S(2)}) collective-permute-start(f32[2,8,128]{2,1,0:T(8,128)S(1)} %pad_maximum_fusion.5), channel_id=1, source_target_pairs={{0,256},{32,288},{64,320},{96,352},{128,384},{160,416},{192,448},{... | collective-permute-start | bytes 24584 | tf_op jit(solution)/shard_map/ppermute | solution.py:215
  172.1 4.8 %collective-permute-start.24 = (bf16[2,128,640]{2,1,0:T(8,128)(2,1)S(1)}, bf16[2,128,640]{2,1,0:T(8,128)(2,1)S(1)}, u32[]{:S(2)}, u32[]{:S(2)}) collective-permute-start(bf16[2,128,640]{2,1,0:T(8,128)(2,1)S(1)} %get-tuple-element.34), channel_id=1, source_target_pairs={{0,16},{1,17},{2,18},{3,19},{4,20},{5,21},{6,22},{7,23},{8,24},{9,... | collective-permute-start | bytes 983048 | tf_op jit(solution)/shard_map/ppermute | solution.py:253
  193.5 13.4 %grams.1 = (f32[8,64,8,128]{3,2,1,0:T(8,128)}, f32[8,64,8,128]{3,2,1,0:T(8,128)}) custom-call(s32[8,8]{1,0:T(8,128)S(1)} %copy-done.18, s32[4]{0:T(128)S(1)} %pad_add_fusion.refs_1_, s32[64,2]{1,0:T(8,128)S(1)} %copy.38.refs_2_, bf16[8,128,640]{2,1,0:T(8,128)(2,1)} %bitcast.134, bf16[8,128,640]{2,1,0:T(8,128)(2,1)} %payouts.3.refs_2_.refs_4_, ...), custom_call_target="tpu_custom_call" | custom-call | flops 1342177280 | bytes 10485760 | tf_op jit(solution)/shard_map/grams/pallas_call | solution.py:182
  208.9 4.3 %collective-permute-done.27 = f32[8,64,8,128]{3,2,1,0:T(8,128)S(1)} collective-permute-done((f32[8,64,8,128]{3,2,1,0:T(8,128)}, f32[8,64,8,128]{3,2,1,0:T(8,128)S(1)}, u32[]{:S(2)}, u32[]{:S(2)}) %collective-permute-start.27) | collective-permute-done | bytes 2097184 | tf_op jit(solution)/shard_map/ppermute | solution.py:229
  218.2 9.8 %collective-permute-start.33 = (f32[64,8,128]{2,1,0:T(8,128)S(1)}, f32[64,8,128]{2,1,0:T(8,128)S(1)}, u32[]{:S(2)}, u32[]{:S(2)}) collective-permute-start(f32[64,8,128]{2,1,0:T(8,128)S(1)} %get-tuple-element.42), channel_id=1, source_target_pairs={{0,384},{32,416},{64,448},{96,480},{128,0},{160,32},{192,64},{224,... | collective-permute-start | bytes 786440 | tf_op jit(solution)/shard_map/ppermute | solution.py:232
  237.0 5.2 %collective-permute-start.34 = (f32[32,8,128]{2,1,0:T(8,128)S(1)}, f32[32,8,128]{2,1,0:T(8,128)S(1)}, u32[]{:S(2)}, u32[]{:S(2)}) collective-permute-start(f32[32,8,128]{2,1,0:T(8,128)S(1)} %get-tuple-element.49), channel_id=1, source_target_pairs={{0,320},{32,352},{64,384},{96,416},{128,448},{160,480},{192,0},{22... | collective-permute-start | bytes 393224 | tf_op jit(solution)/shard_map/ppermute | solution.py:232
  242.2 8.9 %collective-permute-done.32 = f32[64,8,128]{2,1,0:T(8,128)S(1)} collective-permute-done((f32[64,8,128]{2,1,0:T(8,128)S(1)}, f32[64,8,128]{2,1,0:T(8,128)S(1)}, u32[]{:S(2)}, u32[]{:S(2)}) %collective-permute-start.32) | collective-permute-done | bytes 262176 | tf_op jit(solution)/shard_map/ppermute | solution.py:232
  263.1 5.3 %collective-permute-done.31 = f32[64,8,128]{2,1,0:T(8,128)S(1)} collective-permute-done((f32[64,8,128]{2,1,0:T(8,128)S(1)}, f32[64,8,128]{2,1,0:T(8,128)S(1)}, u32[]{:S(2)}, u32[]{:S(2)}) %collective-permute-start.31) | collective-permute-done | bytes 262176 | tf_op jit(solution)/shard_map/ppermute | solution.py:232
  (134 shorter events, 124.3 us)
Async XLA Ops:
  21.0 31.2 %collective-permute-start.8 = (bf16[8,128,640]{2,1,0:T(8,128)(2,1)}, bf16[8,128,640]{2,1,0:T(8,128)(2,1)S(1)}, u32[]{:S(2)}, u32[]{:S(2)}) collective-permute-start(bf16[8,128,640]{2,1,0:T(8,128)(2,1)} %payouts.3.refs_2_.refs_4_), channel_id=1, source_target_pairs={{0,7},{1,0},{2,1},{3,2},{4,3},{5,4},{6,5},{7,6},{8,15},{9,8},{10,9... | collective-permute-start | bytes 3932168 | tf_op jit(solution)/shard_map/ppermute | solution.py:253
  23.5 32.7 %collective-permute-start.4 = (bf16[8,128,640]{2,1,0:T(8,128)(2,1)}, bf16[8,128,640]{2,1,0:T(8,128)(2,1)S(1)}, u32[]{:S(2)}, u32[]{:S(2)}) collective-permute-start(bf16[8,128,640]{2,1,0:T(8,128)(2,1)} %payouts.3.refs_2_.refs_4_), channel_id=1, source_target_pairs={{0,1},{1,2},{2,3},{3,4},{4,5},{5,6},{6,7},{7,0},{8,9},{9,10},{10,1... | collective-permute-start | bytes 3932168 | tf_op jit(solution)/shard_map/ppermute | solution.py:253
  31.8 24.3 %collective-permute-start.5 = (bf16[2,128,640]{2,1,0:T(8,128)(2,1)S(1)}, bf16[2,128,640]{2,1,0:T(8,128)(2,1)S(1)}, u32[]{:S(2)}, u32[]{:S(2)}) collective-permute-start(bf16[2,128,640]{2,1,0:T(8,128)(2,1)S(1)} %get-tuple-element.22), channel_id=1, source_target_pairs={{0,16},{1,17},{2,18},{3,19},{4,20},{5,21},{6,22},{7,23},{8,24},{9,... | collective-permute-start | bytes 983048 | tf_op jit(solution)/shard_map/ppermute | solution.py:253
  35.2 21.0 %collective-permute-start.6 = (bf16[2,128,640]{2,1,0:T(8,128)(2,1)S(1)}, bf16[2,128,640]{2,1,0:T(8,128)(2,1)S(1)}, u32[]{:S(2)}, u32[]{:S(2)}) collective-permute-start(bf16[2,128,640]{2,1,0:T(8,128)(2,1)S(1)} %get-tuple-element.23), channel_id=1, source_target_pairs={{0,8},{1,9},{2,10},{3,11},{4,12},{5,13},{6,14},{7,15},{8,16},{9,17... | collective-permute-start | bytes 983048 | tf_op jit(solution)/shard_map/ppermute | solution.py:253
  52.2 30.3 %collective-permute-start.10 = (bf16[8,128,640]{2,1,0:T(8,128)(2,1)S(1)}, bf16[8,128,640]{2,1,0:T(8,128)(2,1)}, u32[]{:S(2)}, u32[]{:S(2)}) collective-permute-start(bf16[8,128,640]{2,1,0:T(8,128)(2,1)S(1)} %collective-permute-done.8.refs_3_.refs_6_), channel_id=1, source_target_pairs={{0,7},{1,0},{2,1},{3,2},{4,3},{5,4},{6,5},{7,6},{8,15},{9,8},{10,9... | collective-permute-start | bytes 3932168 | tf_op jit(solution)/shard_map/ppermute | solution.py:253
  58.1 31.6 %collective-permute-start.9 = (bf16[8,128,640]{2,1,0:T(8,128)(2,1)}, bf16[8,128,640]{2,1,0:T(8,128)(2,1)S(1)}, u32[]{:S(2)}, u32[]{:S(2)}) collective-permute-start(bf16[8,128,640]{2,1,0:T(8,128)(2,1)} %pass_on.1.refs_2_.refs_5_), channel_id=1, source_target_pairs={{0,1},{1,2},{2,3},{3,4},{4,5},{5,6},{6,7},{7,0},{8,9},{9,10},{10,1... | collective-permute-start | bytes 3932168 | tf_op jit(solution)/shard_map/ppermute | solution.py:253
  68.9 23.5 %collective-permute-start.15 = (bf16[4,128,640]{2,1,0:T(8,128)(2,1)S(1)}, bf16[4,128,640]{2,1,0:T(8,128)(2,1)S(1)}, u32[]{:S(2)}, u32[]{:S(2)}) collective-permute-start(bf16[4,128,640]{2,1,0:T(8,128)(2,1)S(1)} %get-tuple-element.25), channel_id=1, source_target_pairs={{0,16},{1,17},{2,18},{3,19},{4,20},{5,21},{6,22},{7,23},{8,24},{9,... | collective-permute-start | bytes 1966088 | tf_op jit(solution)/shard_map/ppermute | solution.py:253
  72.2 25.9 %collective-permute-start.16 = (bf16[4,128,640]{2,1,0:T(8,128)(2,1)S(1)}, bf16[4,128,640]{2,1,0:T(8,128)(2,1)S(1)}, u32[]{:S(2)}, u32[]{:S(2)}) collective-permute-start(bf16[4,128,640]{2,1,0:T(8,128)(2,1)S(1)} %get-tuple-element.26), channel_id=1, source_target_pairs={{0,8},{1,9},{2,10},{3,11},{4,12},{5,13},{6,14},{7,15},{8,16},{9,17... | collective-permute-start | bytes 1966088 | tf_op jit(solution)/shard_map/ppermute | solution.py:253
  76.2 24.3 %collective-permute-start.17 = (bf16[4,128,640]{2,1,0:T(8,128)(2,1)S(1)}, bf16[4,128,640]{2,1,0:T(8,128)(2,1)S(1)}, u32[]{:S(2)}, u32[]{:S(2)}) collective-permute-start(bf16[4,128,640]{2,1,0:T(8,128)(2,1)S(1)} %get-tuple-element.27), channel_id=1, source_target_pairs={{0,24},{1,25},{2,26},{3,27},{4,28},{5,29},{6,30},{7,31},{8,0},{9,1... | collective-permute-start | bytes 1966088 | tf_op jit(solution)/shard_map/ppermute | solution.py:253
  82.5 32.5 %collective-permute-start.12 = (bf16[8,128,640]{2,1,0:T(8,128)(2,1)}, bf16[8,128,640]{2,1,0:T(8,128)(2,1)S(1)}, u32[]{:S(2)}, u32[]{:S(2)}) collective-permute-start(bf16[8,128,640]{2,1,0:T(8,128)(2,1)} %collective-permute-done.10.refs_3_.refs_8_), channel_id=1, source_target_pairs={{0,7},{1,0},{2,1},{3,2},{4,3},{5,4},{6,5},{7,6},{8,15},{9,8},{10,9... | collective-permute-start | bytes 3932168 | tf_op jit(solution)/shard_map/ppermute | solution.py:253
  89.7 30.4 %collective-permute-start.11 = (bf16[8,128,640]{2,1,0:T(8,128)(2,1)S(1)}, bf16[8,128,640]{2,1,0:T(8,128)(2,1)S(1)}, u32[]{:S(2)}, u32[]{:S(2)}) collective-permute-start(bf16[8,128,640]{2,1,0:T(8,128)(2,1)S(1)} %collective-permute-done.9.refs_2_.refs_7_), channel_id=1, source_target_pairs={{0,1},{1,2},{2,3},{3,4},{4,5},{5,6},{6,7},{7,0},{8,9},{9,10},{10,1... | collective-permute-start | bytes 3932168 | tf_op jit(solution)/shard_map/ppermute | solution.py:253
  105.8 21.0 %collective-permute-start.18 = (bf16[4,128,640]{2,1,0:T(8,128)(2,1)S(1)}, bf16[4,128,640]{2,1,0:T(8,128)(2,1)S(1)}, u32[]{:S(2)}, u32[]{:S(2)}) collective-permute-start(bf16[4,128,640]{2,1,0:T(8,128)(2,1)S(1)} %get-tuple-element.28), channel_id=1, source_target_pairs={{0,16},{1,17},{2,18},{3,19},{4,20},{5,21},{6,22},{7,23},{8,24},{9,... | collective-permute-start | bytes 1966088 | tf_op jit(solution)/shard_map/ppermute | solution.py:253
  109.1 28.3 %collective-permute-start.19 = (bf16[4,128,640]{2,1,0:T(8,128)(2,1)S(1)}, bf16[4,128,640]{2,1,0:T(8,128)(2,1)S(1)}, u32[]{:S(2)}, u32[]{:S(2)}) collective-permute-start(bf16[4,128,640]{2,1,0:T(8,128)(2,1)S(1)} %get-tuple-element.29), channel_id=1, source_target_pairs={{0,8},{1,9},{2,10},{3,11},{4,12},{5,13},{6,14},{7,15},{8,16},{9,17... | collective-permute-start | bytes 1966088 | tf_op jit(solution)/shard_map/ppermute | solution.py:253
  113.0 26.9 %collective-permute-start.20 = (bf16[4,128,640]{2,1,0:T(8,128)(2,1)S(1)}, bf16[4,128,640]{2,1,0:T(8,128)(2,1)S(1)}, u32[]{:S(2)}, u32[]{:S(2)}) collective-permute-start(bf16[4,128,640]{2,1,0:T(8,128)(2,1)S(1)} %get-tuple-element.30), channel_id=1, source_target_pairs={{0,24},{1,25},{2,26},{3,27},{4,28},{5,29},{6,30},{7,31},{8,0},{9,1... | collective-permute-start | bytes 1966088 | tf_op jit(solution)/shard_map/ppermute | solution.py:253
  115.0 32.4 %collective-permute-start.1 = (f32[2,8,128]{2,1,0:T(8,128)S(1)}, f32[2,8,128]{2,1,0:T(8,128)S(1)}, u32[]{:S(2)}, u32[]{:S(2)}) collective-permute-start(f32[2,8,128]{2,1,0:T(8,128)S(1)} %pad_maximum_fusion.3), channel_id=1, source_target_pairs={{0,64},{32,96},{64,128},{96,160},{128,192},{160,224},{192,256},{22... | collective-permute-start | bytes 24584 | tf_op jit(solution)/shard_map/ppermute | solution.py:215
  120.1 41.9 %collective-permute-start.14 = (bf16[8,64,640]{2,1,0:T(8,128)(2,1)S(1)}, bf16[8,64,640]{2,1,0:T(8,128)(2,1)S(1)}, u32[]{:S(2)}, u32[]{:S(2)}) collective-permute-start(bf16[8,64,640]{2,1,0:T(8,128)(2,1)S(1)} %slice.149), channel_id=1, source_target_pairs={{0,7},{1,0},{2,1},{3,2},{4,3},{5,4},{6,5},{7,6},{8,15},{9,8},{10,9... | collective-permute-start | bytes 1966088 | tf_op jit(solution)/shard_map/ppermute | solution.py:253
  126.8 41.9 %collective-permute-start.13 = (bf16[8,64,640]{2,1,0:T(8,128)(2,1)}, bf16[8,64,640]{2,1,0:T(8,128)(2,1)S(1)}, u32[]{:S(2)}, u32[]{:S(2)}) collective-permute-start(bf16[8,64,640]{2,1,0:T(8,128)(2,1)} %slice.148), channel_id=1, source_target_pairs={{0,1},{1,2},{2,3},{3,4},{4,5},{5,6},{6,7},{7,0},{8,9},{9,10},{10,1... | collective-permute-start | bytes 1966088 | tf_op jit(solution)/shard_map/ppermute | solution.py:253
  143.9 36.2 %collective-permute-start.21 = (bf16[4,128,640]{2,1,0:T(8,128)(2,1)}, bf16[4,128,640]{2,1,0:T(8,128)(2,1)}, u32[]{:S(2)}, u32[]{:S(2)}) collective-permute-start(bf16[4,128,640]{2,1,0:T(8,128)(2,1)} %get-tuple-element.31), channel_id=1, source_target_pairs={{0,16},{1,17},{2,18},{3,19},{4,20},{5,21},{6,22},{7,23},{8,24},{9,... | collective-permute-start | bytes 1966088 | tf_op jit(solution)/shard_map/ppermute | solution.py:253
  153.5 32.2 %collective-permute-start.22 = (bf16[4,128,640]{2,1,0:T(8,128)(2,1)}, bf16[4,128,640]{2,1,0:T(8,128)(2,1)}, u32[]{:S(2)}, u32[]{:S(2)}) collective-permute-start(bf16[4,128,640]{2,1,0:T(8,128)(2,1)} %get-tuple-element.32), channel_id=1, source_target_pairs={{0,8},{1,9},{2,10},{3,11},{4,12},{5,13},{6,14},{7,15},{8,16},{9,17... | collective-permute-start | bytes 1966088 | tf_op jit(solution)/shard_map/ppermute | solution.py:253
  160.0 25.7 %collective-permute-start.23 = (bf16[4,128,640]{2,1,0:T(8,128)(2,1)}, bf16[4,128,640]{2,1,0:T(8,128)(2,1)}, u32[]{:S(2)}, u32[]{:S(2)}) collective-permute-start(bf16[4,128,640]{2,1,0:T(8,128)(2,1)} %get-tuple-element.33), channel_id=1, source_target_pairs={{0,24},{1,25},{2,26},{3,27},{4,28},{5,29},{6,30},{7,31},{8,0},{9,1... | collective-permute-start | bytes 1966088 | tf_op jit(solution)/shard_map/ppermute | solution.py:253
  214.7 22.3 %collective-permute-start.28 = (f32[64,8,128]{2,1,0:T(8,128)S(1)}, f32[64,8,128]{2,1,0:T(8,128)S(1)}, u32[]{:S(2)}, u32[]{:S(2)}) collective-permute-start(f32[64,8,128]{2,1,0:T(8,128)S(1)} %get-tuple-element.41), channel_id=1, source_target_pairs={{0,64},{32,96},{64,128},{96,160},{128,192},{160,224},{192,256},{22... | collective-permute-start | bytes 786440 | tf_op jit(solution)/shard_map/ppermute | solution.py:232
  218.2 24.0 %collective-permute-start.33 = (f32[64,8,128]{2,1,0:T(8,128)S(1)}, f32[64,8,128]{2,1,0:T(8,128)S(1)}, u32[]{:S(2)}, u32[]{:S(2)}) collective-permute-start(f32[64,8,128]{2,1,0:T(8,128)S(1)} %get-tuple-element.42), channel_id=1, source_target_pairs={{0,384},{32,416},{64,448},{96,480},{128,0},{160,32},{192,64},{224,... | collective-permute-start | bytes 786440 | tf_op jit(solution)/shard_map/ppermute | solution.py:232
  228.0 23.2 %collective-permute-start.32 = (f32[64,8,128]{2,1,0:T(8,128)S(1)}, f32[64,8,128]{2,1,0:T(8,128)S(1)}, u32[]{:S(2)}, u32[]{:S(2)}) collective-permute-start(f32[64,8,128]{2,1,0:T(8,128)S(1)} %get-tuple-element.43), channel_id=1, source_target_pairs={{0,448},{32,480},{64,0},{96,32},{128,64},{160,96},{192,128},{224,1... | collective-permute-start | bytes 786440 | tf_op jit(solution)/shard_map/ppermute | solution.py:232
  233.3 21.5 %collective-permute-start.30 = (f32[32,8,128]{2,1,0:T(8,128)S(1)}, f32[32,8,128]{2,1,0:T(8,128)S(1)}, u32[]{:S(2)}, u32[]{:S(2)}) collective-permute-start(f32[32,8,128]{2,1,0:T(8,128)S(1)} %get-tuple-element.48), channel_id=1, source_target_pairs={{0,192},{32,224},{64,256},{96,288},{128,320},{160,352},{192,384},{... | collective-permute-start | bytes 393224 | tf_op jit(solution)/shard_map/ppermute | solution.py:232
  (35 other events, 574.5 us)

commit v2 on v1

--- a/solution.py
+++ b/solution.py
@@ -9,7 +9,6 @@
 BLK = 128
 NX, NY, NZ = 4, 8, 8
 FB_DEV = 8
-GATE = 2
 STEPS = (2, 1, 3)
 VMEM_CAP = 48 * 1024 * 1024
 
@@ -32,8 +31,8 @@
 CORE_SWAP = [(i, i ^ 1) for i in range(2 * NZ)]
 
 
-def payout_kernel(first, strike_ref, exit_ref, series_ref, out_ref):
-    b = pl.program_id(0) + first
+def payout_kernel(strike_ref, exit_ref, series_ref, out_ref):
+    b = pl.program_id(0)
     tau = lax.broadcasted_iota(jnp.int32, (BLK, DAY), 1)
     row = lax.broadcasted_iota(jnp.int32, (BLK, DAY), 0)
     upper = jnp.where(row <= tau, 1.0, 0.0).astype(jnp.bfloat16)
@@ -55,38 +54,30 @@
         out_ref[0, :, days] = jnp.where(window_on, value, 0.0).astype(jnp.bfloat16)
 
 
-def payouts(series, strike, leave, first, count, before=None, gate=None):
+def payouts(series, strike, leave):
     rows, days = series.shape
     blocks = rows // BLK
     lines = pl.BlockSpec((blocks, BLK), lambda b: (0, 0))
-    operands = [strike.reshape(blocks, BLK), leave.reshape(blocks, BLK), series]
-    specs = [lines, lines, pl.BlockSpec((BLK, days), lambda b: (b + first, 0))]
-    alias = {}
-    if before is not None:
-        operands += [before, gate]
-        specs += [pl.BlockSpec(memory_space=pl.ANY)] * 2
-        alias = {3: 0}
-    return pl.pallas_call(
-        lambda *refs: payout_kernel(first, *refs[:3], refs[-1]),
-        grid=(count,),
+    return pl.pallas_call(
+        payout_kernel,
+        grid=(blocks,),
         out_shape=jax.ShapeDtypeStruct((blocks, BLK, days), jnp.bfloat16),
-        in_specs=specs,
-        out_specs=pl.BlockSpec((1, BLK, days), lambda b: (b + first, 0, 0)),
-        input_output_aliases=alias,
+        in_specs=[lines, lines, pl.BlockSpec((BLK, days), lambda b: (b, 0))],
+        out_specs=pl.BlockSpec((1, BLK, days), lambda b: (b, 0, 0)),
         name="payouts",
-    )(*operands)
-
-
-def pick_kernel(backs, table_ref, place_ref, *refs):
-    outs, held, sems = refs[-2 - len(STEPS):-2], refs[-2], refs[-1]
+    )(strike.reshape(blocks, BLK), leave.reshape(blocks, BLK), series)
+
+
+def pick_kernel(backs, steps, table_ref, place_ref, *refs):
+    outs, held, sems = refs[-2 - len(steps):-2], refs[-2], refs[-1]
     half = BLK // 2
     copies = []
-    for step, out in zip(STEPS, outs):
+    for step, out in zip(steps, outs):
         x = lax.rem(place_ref[0] + step, NX)
         for i, back in enumerate(backs):
             line = 0 if back is None else lax.rem(place_ref[1] + NY - back, NY)
             for c in range(2):
-                block = table_ref[line, x * 2 + c]
+                block = table_ref[line, (x * NY + place_ref[1]) * 2 + c]
                 n, where = len(copies), out.at[2 * i + c]
                 if refs[0].shape[1] == BLK:
                     copies.append((refs[i].at[block], where, n, 0, BLK))
@@ -107,16 +98,16 @@
         copy.wait()
 
 
-def picks(table, place, sources, backs, gate=()):
+def picks(table, place, sources, backs, steps, gate=()):
     days = sources[0].shape[-1]
     count = 2 * len(backs)
-    number = count * len(STEPS) * (1 if sources[0].shape[1] == BLK else 2)
+    number = count * len(steps) * (1 if sources[0].shape[1] == BLK else 2)
     operands = list(sources) + list(gate)
     return pl.pallas_call(
-        lambda *refs: pick_kernel(backs, *refs),
-        out_shape=[jax.ShapeDtypeStruct((count, BLK, days), jnp.bfloat16)] * len(STEPS),
+        lambda *refs: pick_kernel(backs, steps, *refs),
+        out_shape=[jax.ShapeDtypeStruct((count, BLK, days), jnp.bfloat16)] * len(steps),
         in_specs=[pl.BlockSpec(memory_space=pltpu.SMEM)] * 2 + [pl.BlockSpec(memory_space=pl.ANY)] * len(operands),
-        out_specs=[pl.BlockSpec(memory_space=pl.ANY)] * len(STEPS),
+        out_specs=[pl.BlockSpec(memory_space=pl.ANY)] * len(steps),
         scratch_shapes=[pltpu.VMEM((number, BLK, days), jnp.bfloat16), pltpu.SemaphoreType.DMA((2, number))],
         compiler_params=pltpu.CompilerParams(vmem_limit_bytes=VMEM_CAP),
         cost_estimate=pl.CostEstimate(flops=0, bytes_accessed=number * BLK * days * 4, transcendentals=0),
@@ -127,12 +118,12 @@
 def gram_kernel(factor, table_ref, place_ref, pair_ref, farm_ref, *refs):
     held, relayed = refs[:9], refs[9:24]
     keep_ref, send_ref, slots, sems = refs[24:]
-    x, y, z, core = place_ref[0], place_ref[1], place_ref[2], place_ref[3]
+    x, y, core = place_ref[0], place_ref[1], place_ref[3]
     copies = []
     half = BLK // 2
     for at, back in enumerate((0, 1, 7, 2, 6, 3, 5, 4)):
         for c in range(2):
-            block = table_ref[lax.rem(y + NY - back, NY), x * 2 + c]
+            block = table_ref[lax.rem(y + NY - back, NY), (x * NY + y) * 2 + c]
             if at < 7:
                 copies.append((held[at].at[block], slots.at[0, 2 * at + c]))
             else:
@@ -167,9 +158,8 @@
         for target in range(NZ):
             near_rows = product[target * 16: target * 16 + 8]
             far_rows = product[target * 16 + 8: target * 16 + 16]
-            d = lax.rem(target - z + NZ, NZ)
-            keep_ref[d, p] = jnp.where(core == 0, near_rows, far_rows)
-            send_ref[d, p] = jnp.where(core == 0, far_rows, near_rows)
+            keep_ref[target, p] = jnp.where(core == 0, near_rows, far_rows)
+            send_ref[target, p] = jnp.where(core == 0, far_rows, near_rows)
 
     pl.loop(0, pair_ref.shape[0], unroll=4)(one)
 
@@ -191,19 +181,20 @@
     )(table, place, pairs, farms, *stations)
 
 
-def pass_on(value, after):
+def pass_on(values, after):
     spec = pl.BlockSpec(memory_space=pl.ANY)
     return pl.pallas_call(
         lambda *refs: None,
-        out_shape=jax.ShapeDtypeStruct(value.shape, value.dtype),
-        in_specs=[spec] * (1 + len(after)),
-        out_specs=spec,
-        input_output_aliases={0: 0},
+        out_shape=[jax.ShapeDtypeStruct(v.shape, v.dtype) for v in values],
+        in_specs=[spec] * (len(values) + len(after)),
+        out_specs=[spec] * len(values),
+        input_output_aliases={i: i for i in range(len(values))},
         name="pass_on",
-    )(value, *after)
+    )(*values, *after)
 
 
 def standardised(farm_yield):
+    steps = []
     rows, days = farm_yield.shape
     values = farm_yield.astype(jnp.float32)
     mean = jnp.sum(values, axis=1) / days
@@ -213,6 +204,7 @@
     held = float(days)
     for hop in (CORE_SWAP, z_shift(1), z_shift(2), z_shift(4)):
         other = lax.ppermute(state, "season", hop)
+        steps.append(other)
         gap = other[0] - state[0]
         state = jnp.stack([
             0.5 * (state[0] + other[0]),
@@ -222,26 +214,15 @@
     center = state[0].reshape(rows, 1)
     spread = state[1].reshape(rows, 1) / held
     scaled = ((values - center) * lax.rsqrt(spread + 1e-05)).astype(jnp.bfloat16)
-    return scaled.reshape(rows // BLK, BLK, days)
+    return scaled.reshape(rows // BLK, BLK, days), steps
 
 
 def season_sum(keep, send):
-    other = lax.ppermute(send, "season", CORE_SWAP)
-    part = [keep[d] + other[d] for d in range(NZ)]
-    half = keep.shape[1] // 2
-    hop = lambda v, k: lax.ppermute(v, "season", z_shift(k))
-    up4, down4 = hop(part[4][:half], 3), hop(part[4][half:], -3)
-    up3, down3 = hop(part[3], 2), hop(part[5], -2)
-    up2, down2 = hop(part[2], 1), hop(part[6], -1)
-    right, left = part[1] + up2 + up3, part[7] + down2 + down3
-    right = jnp.concatenate([right[:half] + up4, right[half:]])
-    left = jnp.concatenate([left[:half], left[half:] + down4])
-    total = part[0] + hop(right, 1) + hop(left, -1)
+    part = keep + lax.ppermute(send, "season", CORE_SWAP)
+    lines = [[2 * z + c for z in range(NZ)] for c in range(2)]
+    parts = lax.all_to_all(part.astype(jnp.float16), "season", 0, 0, axis_index_groups=lines, tiled=True)
+    total = jnp.sum(parts.astype(jnp.float32), axis=0)
     return total.transpose(1, 0, 2)
-
-
-def gates(k, relayed, farms):
-    return relayed[k] if 1 <= k < 3 else []
 
 
 def shards(station_index, strike_day, exit_day, farm_yield, send_list, pair_list):
@@ -251,33 +232,38 @@
     place = jnp.stack([farm // NY, farm % NY, season // 2, season % 2]).astype(jnp.int32)
 
     along = lambda v, hop: lax.ppermute(v, "farm", hop)
-    wanted = send_list.reshape(NX, NY, 2).transpose(1, 0, 2)
-    table = lax.all_to_all(wanted, "farm", 0, 0, axis_index_groups=ROWS, tiled=True).reshape(NY, 2 * NX)
-    mine = lax.dynamic_index_in_dim(wanted, farm % NY, 0).reshape(1, 2 * NX)
-
-    blocks = station_index.shape[0] // BLK
-    start = payouts(station_index, strike_day, exit_day, 0, blocks // 2)
-    own = payouts(station_index, strike_day, exit_day, blocks // 2, blocks // 2, start, table)
-
-    farms = standardised(farm_yield)
+    mine = send_list.reshape(1, -1)
+    table = lax.all_to_all(
+        jnp.broadcast_to(mine, (NY, mine.shape[1])), "farm", 0, 0, axis_index_groups=ROWS, tiled=True)
+    own = payouts(station_index, strike_day, exit_day)
+    own, = pass_on([own], [table])
+
+    farms, steps = standardised(farm_yield)
 
     relayed = []
 
-    def relay(table, sources, backs, gate=()):
-        chosen = picks(table, place, sources, backs, gate)
-        relayed.append([along(v, x_shift(step)) for v, step in zip(chosen, STEPS)])
+    def relay(table, sources, backs, gates=((), ())):
+        arrived = []
+        for steps, gate in zip((STEPS[:1], STEPS[1:]), gates):
+            chosen = picks(table, place, sources, backs, steps, gate)
+            arrived += [along(v, x_shift(step)) for v, step in zip(chosen, steps)]
+        relayed.append(arrived)
+
+    def before(also=()):
+        return relayed[-1][:1] + list(also), relayed[-1][1:]
 
     half = BLK // 2
     relay(mine, [own], (None,))
     ups, downs = [along(own, y_shift(1))], [along(own, y_shift(-1))]
-    ups[0] = pass_on(ups[0], relayed[0])
-    for _ in range(2):
-        ups.append(along(ups[-1], y_shift(1)))
-        downs.append(along(downs[-1], y_shift(-1)))
+    ups[0], = pass_on([ups[0]], relayed[0] + steps[:1])
+    for k in range(3):
+        relay(table, [ups[k], downs[k]], (k + 1, NY - k - 1), before(steps[k:k + 1]) if k else ((), ()))
+        if k < 2:
+            ups.append(along(ups[k], y_shift(1)))
+            downs.append(along(downs[k], y_shift(-1)))
+            ups[k + 1], = pass_on([ups[k + 1]], relayed[k + 1][1:] if k == 0 else relayed[k + 1][:1])
     far = [along(ups[2][:, :half], y_shift(1)), along(downs[2][:, half:], y_shift(-1))]
-    for k in range(3):
-        relay(table, [ups[k], downs[k]], (k + 1, NY - k - 1), gates(k, relayed, farms))
-    relay(table, far, (NY // 2,), gates(3, relayed, farms))
+    relay(table, far, (NY // 2,))
 
     held = [own] + [v for k in range(3) for v in (ups[k], downs[k])] + far
     stations = held + [v for group in relayed for v in group]

time: 272 us -> 247 us (0.908)
  blocking collectives: 0 us -> 35.5 us
  waiting for transfers between devices: 74.3 us -> 38.9 us
  starting transfers between devices: 134 us -> 103 us
  local copies, waits for them, and re-layouts: 9.94 us -> 14.8 us
    all_to_all x0 -> x1, blocking collectives: none -> 35.5 us  [season_sum(): lax.all_to_all(part.astype(jnp.float16), 'season', 0, 0, axis_index_group...]
    ppermute x9 -> x1, starting transfers between devices: 35.2 us -> 1.92 us  [season_sum(): part = keep + lax.ppermute(send, 'season', CORE_SWAP)]
    ppermute x23, waiting for transfers between devices: 44.7 us -> 24.2 us  [shards(): along = lambda v, hop: lax.ppermute(v, 'farm', hop)]
    ppermute x9 -> x1, waiting for transfers between devices: 23.4 us -> 4.34 us  [season_sum(): part = keep + lax.ppermute(send, 'season', CORE_SWAP)]
    ppermute x4, waiting for transfers between devices: 2.53 us -> 9.68 us  [standardised(): other = lax.ppermute(state, 'season', hop)]
    unnamed x45 -> x56, local copies, waits for them, and re-layouts: 5.71 us -> 10.1 us
    ppermute x23, starting transfers between devices: 72.7 us -> 75.9 us  [shards(): along = lambda v, hop: lax.ppermute(v, 'farm', hop)]
    all_to_all x1, waiting for transfers between devices: 3.69 us -> 0.71 us  [shards(): lax.all_to_all(jnp.broadcast_to(mine, (NY, mine.shape[1])), 'farm', 0, 0,...]
  transfers between devices with their start and end apart: 37 -> 29, of which waited for: 20 -> 10; matrix products, arithmetic and copies ran while one was open for 2% -> 3% of each run, Pallas kernels for 10% -> 13%
where the time goes in v2:
time: 247 us; the launch traced here: 246 us
  starting transfers between devices  103 us (42%)
  Pallas kernels  46.2 us (19%)
  waiting for transfers between devices  38.9 us (16%)
  blocking collectives  35.5 us (14%)
  local copies, waits for them, and re-layouts  14.8 us (6%)
  other arithmetic  7.03 us (3%)
    ppermute x23, starting transfers between devices, shards(): along = lambda v, hop: lax.ppermute(v, 'farm', hop)  75.9 us
    all_to_all x1, blocking collectives, season_sum(): lax.all_to_all(part.astype(jnp.float16), 'season', 0, 0, axis_index_group...  35.5 us
    pallas_call x10, Pallas kernels, picks(): pl.pallas_call(lambda *refs: pick_kernel(backs, steps, *refs), out_shape=...  26 us
    ppermute x23, waiting for transfers between devices, shards(): along = lambda v, hop: lax.ppermute(v, 'farm', hop)  24.2 us
    ppermute x4, starting transfers between devices, standardised(): other = lax.ppermute(state, 'season', hop)  17.7 us
    pallas_call x1, Pallas kernels, grams(): pl.pallas_call(lambda *refs: gram_kernel(factor, *refs), out_shape=[shape...  13.3 us
    unnamed x56, local copies, waits for them, and re-layouts  10.1 us
    ppermute x4, waiting for transfers between devices, standardised(): other = lax.ppermute(state, 'season', hop)  9.68 us
  transfers between devices with their start and end apart: 29, of which 10 were waited for; matrix products, arithmetic and copies ran while one was open for 3% of the time, Pallas kernels for 13%

profile of v2, /device:TPU:6, one launch (start us, length us, event | category | flops | bytes accessed | tf_op | source)
XLA Modules:
  0.0 245.9 jit_solution(2114803531047578764)
XLA Ops:
  1.5 7.1 %all-to-all-start = ((s32[8,1,64]{2,1,0:T(1,128)}), s32[8,1,64]{2,1,0:T(1,128)S(1)}, u32[]{:S(2)}, u32[]{:S(2)}) async-start(s32[8,1,64]{2,1,0:T(1,128)} %broadcast_in_dim.9), calls=%async_computation | async-start | bytes 8192 | tf_op jit(solution)/shard_map/all_to_all | solution.py:236
  8.6 6.9 %payouts.1.refs_0_ = bf16[8,128,640]{2,1,0:T(8,128)(2,1)} custom-call(s32[8,128]{1,0:T(8,128)} %bitcast.109, s32[8,128]{1,0:T(8,128)} %bitcast.110, bf16[1024,640]{1,0:T(8,128)(2,1)} %series_ref.1), custom_call_target="tpu_custom_call" | custom-call | tf_op jit(solution)/shard_map/payouts/pallas_call | solution.py:61
  16.8 4.5 %collective-permute-start.8 = (bf16[8,128,640]{2,1,0:T(8,128)(2,1)}, bf16[8,128,640]{2,1,0:T(8,128)(2,1)}, u32[]{:S(2)}, u32[]{:S(2)}) collective-permute-start(bf16[8,128,640]{2,1,0:T(8,128)(2,1)} %pass_on.4.refs_2_.refs_4_), channel_id=1, source_target_pairs={{0,7},{1,0},{2,1},{3,2},{4,3},{5,4},{6,5},{7,6},{8,15},{9,8},{10,9... | collective-permute-start | bytes 3932168 | tf_op jit(solution)/shard_map/ppermute | solution.py:234
  35.9 4.0 %collective-permute-start.6 = (bf16[2,128,640]{2,1,0:T(8,128)(2,1)S(1)}, bf16[2,128,640]{2,1,0:T(8,128)(2,1)S(1)}, u32[]{:S(2)}, u32[]{:S(2)}) collective-permute-start(bf16[2,128,640]{2,1,0:T(8,128)(2,1)S(1)} %get-tuple-element.17), channel_id=1, source_target_pairs={{0,8},{1,9},{2,10},{3,11},{4,12},{5,13},{6,14},{7,15},{8,16},{9,17... | collective-permute-start | bytes 983048 | tf_op jit(solution)/shard_map/ppermute | solution.py:234
  41.9 7.2 %collective-permute-done.8.refs_3_.refs_6_ = bf16[8,128,640]{2,1,0:T(8,128)(2,1)} collective-permute-done((bf16[8,128,640]{2,1,0:T(8,128)(2,1)}, bf16[8,128,640]{2,1,0:T(8,128)(2,1)}, u32[]{:S(2)}, u32[]{:S(2)}) %collective-permute-start.8) | collective-permute-done | bytes 1310752 | tf_op jit(solution)/shard_map/ppermute | solution.py:234
  49.1 5.6 %collective-permute-start.12 = (bf16[8,128,640]{2,1,0:T(8,128)(2,1)}, bf16[8,128,640]{2,1,0:T(8,128)(2,1)}, u32[]{:S(2)}, u32[]{:S(2)}) collective-permute-start(bf16[8,128,640]{2,1,0:T(8,128)(2,1)} %collective-permute-done.8.refs_3_.refs_6_), channel_id=1, source_target_pairs={{0,7},{1,0},{2,1},{3,2},{4,3},{5,4},{6,5},{7,6},{8,15},{9,8},{10,9... | collective-permute-start | bytes 3932168 | tf_op jit(solution)/shard_map/ppermute | solution.py:234
  60.0 3.4 %picks.12 = (bf16[4,128,640]{2,1,0:T(8,128)(2,1)S(1)}, bf16[4,128,640]{2,1,0:T(8,128)(2,1)S(1)}) custom-call(s32[8,64]{1,0:T(8,128)S(1)} %bitcast.97, s32[4]{0:T(128)S(1)} %pad_add_fusion.refs_1_, bf16[8,128,640]{2,1,0:T(8,128)(2,1)S(1)} %copy-done.6, bf16[8,128,640]{2,1,0:T(8,128)(2,1)} %collective-permute-done.8.refs_3_.refs_6_), custom_call_target="tpu_custom_call" | custom-call | bytes 2621440 | tf_op jit(solution)/shard_map/picks/pallas_call | solution.py:106
  72.1 9.4 %collective-permute-done.12.refs_3_.refs_8_ = bf16[8,128,640]{2,1,0:T(8,128)(2,1)} collective-permute-done((bf16[8,128,640]{2,1,0:T(8,128)(2,1)}, bf16[8,128,640]{2,1,0:T(8,128)(2,1)}, u32[]{:S(2)}, u32[]{:S(2)}) %collective-permute-start.12) | collective-permute-done | bytes 1310752 | tf_op jit(solution)/shard_map/ppermute | solution.py:234
  81.5 5.6 %collective-permute-start.16 = (bf16[8,128,640]{2,1,0:T(8,128)(2,1)}, bf16[8,128,640]{2,1,0:T(8,128)(2,1)S(1)}, u32[]{:S(2)}, u32[]{:S(2)}) collective-permute-start(bf16[8,128,640]{2,1,0:T(8,128)(2,1)} %collective-permute-done.12.refs_3_.refs_8_), channel_id=1, source_target_pairs={{0,7},{1,0},{2,1},{3,2},{4,3},{5,4},{6,5},{7,6},{8,15},{9,8},{10,9... | collective-permute-start | bytes 3932168 | tf_op jit(solution)/shard_map/ppermute | solution.py:234
  94.3 4.3 %collective-permute-start.1 = (f32[2,8,128]{2,1,0:T(8,128)S(1)}, f32[2,8,128]{2,1,0:T(8,128)S(1)}, u32[]{:S(2)}, u32[]{:S(2)}) collective-permute-start(f32[2,8,128]{2,1,0:T(8,128)S(1)} %pad_maximum_fusion.1), channel_id=1, source_target_pairs={{0,64},{32,96},{64,128},{96,160},{128,192},{160,224},{192,256},{22... | collective-permute-start | bytes 24584 | tf_op jit(solution)/shard_map/ppermute | solution.py:206
  98.6 8.3 %collective-permute-done.1.refs_5_ = f32[2,8,128]{2,1,0:T(8,128)S(1)} collective-permute-done((f32[2,8,128]{2,1,0:T(8,128)S(1)}, f32[2,8,128]{2,1,0:T(8,128)S(1)}, u32[]{:S(2)}, u32[]{:S(2)}) %collective-permute-start.1) | collective-permute-done | bytes 8224 | tf_op jit(solution)/shard_map/ppermute | solution.py:206
  110.6 4.0 %collective-permute-start.15 = (bf16[4,128,640]{2,1,0:T(8,128)(2,1)S(1)}, bf16[4,128,640]{2,1,0:T(8,128)(2,1)S(1)}, u32[]{:S(2)}, u32[]{:S(2)}) collective-permute-start(bf16[4,128,640]{2,1,0:T(8,128)(2,1)S(1)} %picks.14), channel_id=1, source_target_pairs={{0,16},{1,17},{2,18},{3,19},{4,20},{5,21},{6,22},{7,23},{8,24},{9,... | collective-permute-start | bytes 1966088 | tf_op jit(solution)/shard_map/ppermute | solution.py:234
  114.7 3.4 %picks.15 = (bf16[4,128,640]{2,1,0:T(8,128)(2,1)}, bf16[4,128,640]{2,1,0:T(8,128)(2,1)}) custom-call(s32[8,64]{1,0:T(8,128)S(1)} %bitcast.100, s32[4]{0:T(128)S(1)} %pad_add_fusion.refs_1_, bf16[8,128,640]{2,1,0:T(8,128)(2,1)S(1)} %copy-done.4, bf16[8,128,640]{2,1,0:T(8,128)(2,1)} %collective-permute-done.12.refs_3_.refs_8_, ...), custom_call_target="tpu_custom_call" | custom-call | bytes 2621440 | tf_op jit(solution)/shard_map/picks/pallas_call | solution.py:106
  120.5 3.5 %collective-permute-start.20 = (bf16[4,128,640]{2,1,0:T(8,128)(2,1)}, bf16[4,128,640]{2,1,0:T(8,128)(2,1)}, u32[]{:S(2)}, u32[]{:S(2)}) collective-permute-start(bf16[4,128,640]{2,1,0:T(8,128)(2,1)} %get-tuple-element.22), channel_id=1, source_target_pairs={{0,24},{1,25},{2,26},{3,27},{4,28},{5,29},{6,30},{7,31},{8,0},{9,1... | collective-permute-start | bytes 1966088 | tf_op jit(solution)/shard_map/ppermute | solution.py:234
  125.0 5.1 %collective-permute-start.18 = (bf16[8,64,640]{2,1,0:T(8,128)(2,1)}, bf16[8,64,640]{2,1,0:T(8,128)(2,1)}, u32[]{:S(2)}, u32[]{:S(2)}) collective-permute-start(bf16[8,64,640]{2,1,0:T(8,128)(2,1)} %slice.53), channel_id=1, source_target_pairs={{0,7},{1,0},{2,1},{3,2},{4,3},{5,4},{6,5},{7,6},{8,15},{9,8},{10,9... | collective-permute-start | bytes 1966088 | tf_op jit(solution)/shard_map/ppermute | solution.py:234
  131.7 3.8 %collective-permute-start.2 = (f32[2,8,128]{2,1,0:T(8,128)S(1)}, f32[2,8,128]{2,1,0:T(8,128)S(1)}, u32[]{:S(2)}, u32[]{:S(2)}) collective-permute-start(f32[2,8,128]{2,1,0:T(8,128)S(1)} %pad_maximum_fusion.2), channel_id=1, source_target_pairs={{0,128},{32,160},{64,192},{96,224},{128,256},{160,288},{192,320},{... | collective-permute-start | bytes 24584 | tf_op jit(solution)/shard_map/ppermute | solution.py:206
  148.7 3.3 %picks.17 = (bf16[4,128,640]{2,1,0:T(8,128)(2,1)}, bf16[4,128,640]{2,1,0:T(8,128)(2,1)S(1)}) custom-call(s32[8,64]{1,0:T(8,128)S(1)} %bitcast.102, s32[4]{0:T(128)S(1)} %pad_add_fusion.refs_1_, bf16[8,128,640]{2,1,0:T(8,128)(2,1)S(1)} %copy-done.2, bf16[8,128,640]{2,1,0:T(8,128)(2,1)S(1)} %collective-permute-done.16.refs_3_.refs_10_, ...), custom_call_target="tpu_custom_call" | custom-call | bytes 2621440 | tf_op jit(solution)/shard_map/picks/pallas_call | solution.py:106
  152.0 4.2 %collective-permute-start.22 = (bf16[4,128,640]{2,1,0:T(8,128)(2,1)}, bf16[4,128,640]{2,1,0:T(8,128)(2,1)S(1)}, u32[]{:S(2)}, u32[]{:S(2)}) collective-permute-start(bf16[4,128,640]{2,1,0:T(8,128)(2,1)} %get-tuple-element.23), channel_id=1, source_target_pairs={{0,8},{1,9},{2,10},{3,11},{4,12},{5,13},{6,14},{7,15},{8,16},{9,17... | collective-permute-start | bytes 1966088 | tf_op jit(solution)/shard_map/ppermute | solution.py:234
  158.2 7.7 %collective-permute-start.3 = (f32[2,8,128]{2,1,0:T(8,128)S(1)}, f32[2,8,128]{2,1,0:T(8,128)S(1)}, u32[]{:S(2)}, u32[]{:S(2)}) collective-permute-start(f32[2,8,128]{2,1,0:T(8,128)S(1)} %pad_maximum_fusion.3), channel_id=1, source_target_pairs={{0,256},{32,288},{64,320},{96,352},{128,384},{160,416},{192,448},{... | collective-permute-start | bytes 24584 | tf_op jit(solution)/shard_map/ppermute | solution.py:206
  168.0 3.9 %collective-permute-start.24 = (bf16[2,128,640]{2,1,0:T(8,128)(2,1)S(1)}, bf16[2,128,640]{2,1,0:T(8,128)(2,1)S(1)}, u32[]{:S(2)}, u32[]{:S(2)}) collective-permute-start(bf16[2,128,640]{2,1,0:T(8,128)(2,1)S(1)} %picks.18), channel_id=1, source_target_pairs={{0,16},{1,17},{2,18},{3,19},{4,20},{5,21},{6,22},{7,23},{8,24},{9,... | collective-permute-start | bytes 983048 | tf_op jit(solution)/shard_map/ppermute | solution.py:234
  184.1 3.9 %collective-permute-done.26.refs_27_ = bf16[2,128,640]{2,1,0:T(8,128)(2,1)S(1)} collective-permute-done((bf16[2,128,640]{2,1,0:T(8,128)(2,1)S(1)}, bf16[2,128,640]{2,1,0:T(8,128)(2,1)S(1)}, u32[]{:S(2)}, u32[]{:S(2)}) %collective-permute-start.26) | collective-permute-done | bytes 327712 | tf_op jit(solution)/shard_map/ppermute | solution.py:234
  188.0 13.3 %grams.1 = (f32[8,64,8,128]{3,2,1,0:T(8,128)}, f32[8,64,8,128]{3,2,1,0:T(8,128)}) custom-call(s32[8,64]{1,0:T(8,128)S(1)} %bitcast.105, s32[4]{0:T(128)S(1)} %pad_add_fusion.refs_1_, s32[64,2]{1,0:T(8,128)S(1)} %copy.19.refs_2_, bf16[8,128,640]{2,1,0:T(8,128)(2,1)} %bitcast.106, bf16[8,128,640]{2,1,0:T(8,128)(2,1)} %pass_on.4.refs_2_.refs_4_, ...), custom_call_target="tpu_custom_call" | custom-call | flops 1342177280 | bytes 10485760 | tf_op jit(solution)/shard_map/grams/pallas_call | solution.py:172
  203.2 4.3 %collective-permute-done.27 = f32[8,64,8,128]{3,2,1,0:T(8,128)S(1)} collective-permute-done((f32[8,64,8,128]{3,2,1,0:T(8,128)}, f32[8,64,8,128]{3,2,1,0:T(8,128)S(1)}, u32[]{:S(2)}, u32[]{:S(2)}) %collective-permute-start.27) | collective-permute-done | bytes 2097184 | tf_op jit(solution)/shard_map/ppermute | solution.py:221
  209.4 35.5 %all_to_all.13 = f16[8,64,8,128]{3,2,1,0:T(8,128)(2,1)S(1)} all-to-all(f16[8,64,8,128]{3,2,1,0:T(8,128)(2,1)S(1)} %add_convert_fusion), channel_id=1, replica_groups={{0,64,128,192,256,320,384,448},{32,96,160,224,288,352,416,480},{1,65,12..., dimensions={0} | all-to-all | bytes 2097152 | tf_op jit(solution)/shard_map/all_to_all | solution.py:223
  (128 shorter events, 82.7 us)
Async XLA Ops:
  1.5 14.7 %all-to-all-start = ((s32[8,1,64]{2,1,0:T(1,128)}), s32[8,1,64]{2,1,0:T(1,128)S(1)}, u32[]{:S(2)}, u32[]{:S(2)}) async-start(s32[8,1,64]{2,1,0:T(1,128)} %broadcast_in_dim.9), calls=%async_computation | async-start | bytes 8192 | tf_op jit(solution)/shard_map/all_to_all | solution.py:236
  16.8 32.3 %collective-permute-start.8 = (bf16[8,128,640]{2,1,0:T(8,128)(2,1)}, bf16[8,128,640]{2,1,0:T(8,128)(2,1)}, u32[]{:S(2)}, u32[]{:S(2)}) collective-permute-start(bf16[8,128,640]{2,1,0:T(8,128)(2,1)} %pass_on.4.refs_2_.refs_4_), channel_id=1, source_target_pairs={{0,7},{1,0},{2,1},{3,2},{4,3},{5,4},{6,5},{7,6},{8,15},{9,8},{10,9... | collective-permute-start | bytes 3932168 | tf_op jit(solution)/shard_map/ppermute | solution.py:234
  21.3 33.4 %collective-permute-start.4 = (bf16[8,128,640]{2,1,0:T(8,128)(2,1)}, bf16[8,128,640]{2,1,0:T(8,128)(2,1)S(1)}, u32[]{:S(2)}, u32[]{:S(2)}) collective-permute-start(bf16[8,128,640]{2,1,0:T(8,128)(2,1)} %pass_on.4.refs_2_.refs_4_), channel_id=1, source_target_pairs={{0,1},{1,2},{2,3},{3,4},{4,5},{5,6},{6,7},{7,0},{8,9},{9,10},{10,1... | collective-permute-start | bytes 3932168 | tf_op jit(solution)/shard_map/ppermute | solution.py:234
  26.7 13.3 %collective-permute-start = (f32[2,8,128]{2,1,0:T(8,128)S(1)}, f32[2,8,128]{2,1,0:T(8,128)S(1)}, u32[]{:S(2)}, u32[]{:S(2)}) collective-permute-start(f32[2,8,128]{2,1,0:T(8,128)S(1)} %pad_maximum_fusion), channel_id=1, source_target_pairs={{0,32},{32,0},{64,96},{96,64},{128,160},{160,128},{192,224},{224,1... | collective-permute-start | bytes 24584 | tf_op jit(solution)/shard_map/ppermute | solution.py:206
  32.6 22.1 %collective-permute-start.5 = (bf16[2,128,640]{2,1,0:T(8,128)(2,1)S(1)}, bf16[2,128,640]{2,1,0:T(8,128)(2,1)S(1)}, u32[]{:S(2)}, u32[]{:S(2)}) collective-permute-start(bf16[2,128,640]{2,1,0:T(8,128)(2,1)S(1)} %picks.10), channel_id=1, source_target_pairs={{0,16},{1,17},{2,18},{3,19},{4,20},{5,21},{6,22},{7,23},{8,24},{9,... | collective-permute-start | bytes 983048 | tf_op jit(solution)/shard_map/ppermute | solution.py:234
  35.9 18.8 %collective-permute-start.6 = (bf16[2,128,640]{2,1,0:T(8,128)(2,1)S(1)}, bf16[2,128,640]{2,1,0:T(8,128)(2,1)S(1)}, u32[]{:S(2)}, u32[]{:S(2)}) collective-permute-start(bf16[2,128,640]{2,1,0:T(8,128)(2,1)S(1)} %get-tuple-element.17), channel_id=1, source_target_pairs={{0,8},{1,9},{2,10},{3,11},{4,12},{5,13},{6,14},{7,15},{8,16},{9,17... | collective-permute-start | bytes 983048 | tf_op jit(solution)/shard_map/ppermute | solution.py:234
  40.0 14.8 %collective-permute-start.7 = (bf16[2,128,640]{2,1,0:T(8,128)(2,1)S(1)}, bf16[2,128,640]{2,1,0:T(8,128)(2,1)S(1)}, u32[]{:S(2)}, u32[]{:S(2)}) collective-permute-start(bf16[2,128,640]{2,1,0:T(8,128)(2,1)S(1)} %get-tuple-element.18), channel_id=1, source_target_pairs={{0,24},{1,25},{2,26},{3,27},{4,28},{5,29},{6,30},{7,31},{8,0},{9,1... | collective-permute-start | bytes 983048 | tf_op jit(solution)/shard_map/ppermute | solution.py:234
  49.1 32.4 %collective-permute-start.12 = (bf16[8,128,640]{2,1,0:T(8,128)(2,1)}, bf16[8,128,640]{2,1,0:T(8,128)(2,1)}, u32[]{:S(2)}, u32[]{:S(2)}) collective-permute-start(bf16[8,128,640]{2,1,0:T(8,128)(2,1)} %collective-permute-done.8.refs_3_.refs_6_), channel_id=1, source_target_pairs={{0,7},{1,0},{2,1},{3,2},{4,3},{5,4},{6,5},{7,6},{8,15},{9,8},{10,9... | collective-permute-start | bytes 3932168 | tf_op jit(solution)/shard_map/ppermute | solution.py:234
  56.7 33.7 %collective-permute-start.9 = (bf16[8,128,640]{2,1,0:T(8,128)(2,1)}, bf16[8,128,640]{2,1,0:T(8,128)(2,1)S(1)}, u32[]{:S(2)}, u32[]{:S(2)}) collective-permute-start(bf16[8,128,640]{2,1,0:T(8,128)(2,1)} %pass_on.5.refs_2_.refs_5_), channel_id=1, source_target_pairs={{0,1},{1,2},{2,3},{3,4},{4,5},{5,6},{6,7},{7,0},{8,9},{9,10},{10,1... | collective-permute-start | bytes 3932168 | tf_op jit(solution)/shard_map/ppermute | solution.py:234
  63.3 27.1 %collective-permute-start.10 = (bf16[4,128,640]{2,1,0:T(8,128)(2,1)S(1)}, bf16[4,128,640]{2,1,0:T(8,128)(2,1)S(1)}, u32[]{:S(2)}, u32[]{:S(2)}) collective-permute-start(bf16[4,128,640]{2,1,0:T(8,128)(2,1)S(1)} %get-tuple-element.19), channel_id=1, source_target_pairs={{0,8},{1,9},{2,10},{3,11},{4,12},{5,13},{6,14},{7,15},{8,16},{9,17... | collective-permute-start | bytes 1966088 | tf_op jit(solution)/shard_map/ppermute | solution.py:234
  66.3 24.1 %collective-permute-start.11 = (bf16[4,128,640]{2,1,0:T(8,128)(2,1)S(1)}, bf16[4,128,640]{2,1,0:T(8,128)(2,1)}, u32[]{:S(2)}, u32[]{:S(2)}) collective-permute-start(bf16[4,128,640]{2,1,0:T(8,128)(2,1)S(1)} %get-tuple-element.20), channel_id=1, source_target_pairs={{0,24},{1,25},{2,26},{3,27},{4,28},{5,29},{6,30},{7,31},{8,0},{9,1... | collective-permute-start | bytes 1966088 | tf_op jit(solution)/shard_map/ppermute | solution.py:234
  81.5 42.5 %collective-permute-start.16 = (bf16[8,128,640]{2,1,0:T(8,128)(2,1)}, bf16[8,128,640]{2,1,0:T(8,128)(2,1)S(1)}, u32[]{:S(2)}, u32[]{:S(2)}) collective-permute-start(bf16[8,128,640]{2,1,0:T(8,128)(2,1)} %collective-permute-done.12.refs_3_.refs_8_), channel_id=1, source_target_pairs={{0,7},{1,0},{2,1},{3,2},{4,3},{5,4},{6,5},{7,6},{8,15},{9,8},{10,9... | collective-permute-start | bytes 3932168 | tf_op jit(solution)/shard_map/ppermute | solution.py:234
  87.1 19.8 %collective-permute-start.14 = (bf16[4,128,640]{2,1,0:T(8,128)(2,1)}, bf16[4,128,640]{2,1,0:T(8,128)(2,1)}, u32[]{:S(2)}, u32[]{:S(2)}) collective-permute-start(bf16[4,128,640]{2,1,0:T(8,128)(2,1)} %picks.13), channel_id=1, source_target_pairs={{0,16},{1,17},{2,18},{3,19},{4,20},{5,21},{6,22},{7,23},{8,24},{9,... | collective-permute-start | bytes 1966088 | tf_op jit(solution)/shard_map/ppermute | solution.py:234
  92.4 43.2 %collective-permute-start.13 = (bf16[8,128,640]{2,1,0:T(8,128)(2,1)}, bf16[8,128,640]{2,1,0:T(8,128)(2,1)S(1)}, u32[]{:S(2)}, u32[]{:S(2)}) collective-permute-start(bf16[8,128,640]{2,1,0:T(8,128)(2,1)} %pass_on.6.refs_2_.refs_7_), channel_id=1, source_target_pairs={{0,1},{1,2},{2,3},{3,4},{4,5},{5,6},{6,7},{7,0},{8,9},{9,10},{10,1... | collective-permute-start | bytes 3932168 | tf_op jit(solution)/shard_map/ppermute | solution.py:234
  110.6 21.1 %collective-permute-start.15 = (bf16[4,128,640]{2,1,0:T(8,128)(2,1)S(1)}, bf16[4,128,640]{2,1,0:T(8,128)(2,1)S(1)}, u32[]{:S(2)}, u32[]{:S(2)}) collective-permute-start(bf16[4,128,640]{2,1,0:T(8,128)(2,1)S(1)} %picks.14), channel_id=1, source_target_pairs={{0,16},{1,17},{2,18},{3,19},{4,20},{5,21},{6,22},{7,23},{8,24},{9,... | collective-permute-start | bytes 1966088 | tf_op jit(solution)/shard_map/ppermute | solution.py:234
  118.1 30.5 %collective-permute-start.19 = (bf16[4,128,640]{2,1,0:T(8,128)(2,1)}, bf16[4,128,640]{2,1,0:T(8,128)(2,1)}, u32[]{:S(2)}, u32[]{:S(2)}) collective-permute-start(bf16[4,128,640]{2,1,0:T(8,128)(2,1)} %get-tuple-element.21), channel_id=1, source_target_pairs={{0,8},{1,9},{2,10},{3,11},{4,12},{5,13},{6,14},{7,15},{8,16},{9,17... | collective-permute-start | bytes 1966088 | tf_op jit(solution)/shard_map/ppermute | solution.py:234
  120.5 28.1 %collective-permute-start.20 = (bf16[4,128,640]{2,1,0:T(8,128)(2,1)}, bf16[4,128,640]{2,1,0:T(8,128)(2,1)}, u32[]{:S(2)}, u32[]{:S(2)}) collective-permute-start(bf16[4,128,640]{2,1,0:T(8,128)(2,1)} %get-tuple-element.22), channel_id=1, source_target_pairs={{0,24},{1,25},{2,26},{3,27},{4,28},{5,29},{6,30},{7,31},{8,0},{9,1... | collective-permute-start | bytes 1966088 | tf_op jit(solution)/shard_map/ppermute | solution.py:234
  125.0 33.2 %collective-permute-start.18 = (bf16[8,64,640]{2,1,0:T(8,128)(2,1)}, bf16[8,64,640]{2,1,0:T(8,128)(2,1)}, u32[]{:S(2)}, u32[]{:S(2)}) collective-permute-start(bf16[8,64,640]{2,1,0:T(8,128)(2,1)} %slice.53), channel_id=1, source_target_pairs={{0,7},{1,0},{2,1},{3,2},{4,3},{5,4},{6,5},{7,6},{8,15},{9,8},{10,9... | collective-permute-start | bytes 1966088 | tf_op jit(solution)/shard_map/ppermute | solution.py:234
  138.7 27.4 %collective-permute-start.17 = (bf16[8,64,640]{2,1,0:T(8,128)(2,1)}, bf16[8,64,640]{2,1,0:T(8,128)(2,1)S(1)}, u32[]{:S(2)}, u32[]{:S(2)}) collective-permute-start(bf16[8,64,640]{2,1,0:T(8,128)(2,1)} %slice.52), channel_id=1, source_target_pairs={{0,1},{1,2},{2,3},{3,4},{4,5},{5,6},{6,7},{7,0},{8,9},{9,10},{10,1... | collective-permute-start | bytes 1966088 | tf_op jit(solution)/shard_map/ppermute | solution.py:234
  145.5 32.1 %collective-permute-start.21 = (bf16[4,128,640]{2,1,0:T(8,128)(2,1)S(1)}, bf16[4,128,640]{2,1,0:T(8,128)(2,1)}, u32[]{:S(2)}, u32[]{:S(2)}) collective-permute-start(bf16[4,128,640]{2,1,0:T(8,128)(2,1)S(1)} %picks.16), channel_id=1, source_target_pairs={{0,16},{1,17},{2,18},{3,19},{4,20},{5,21},{6,22},{7,23},{8,24},{9,... | collective-permute-start | bytes 1966088 | tf_op jit(solution)/shard_map/ppermute | solution.py:234
  152.0 30.0 %collective-permute-start.22 = (bf16[4,128,640]{2,1,0:T(8,128)(2,1)}, bf16[4,128,640]{2,1,0:T(8,128)(2,1)S(1)}, u32[]{:S(2)}, u32[]{:S(2)}) collective-permute-start(bf16[4,128,640]{2,1,0:T(8,128)(2,1)} %get-tuple-element.23), channel_id=1, source_target_pairs={{0,8},{1,9},{2,10},{3,11},{4,12},{5,13},{6,14},{7,15},{8,16},{9,17... | collective-permute-start | bytes 1966088 | tf_op jit(solution)/shard_map/ppermute | solution.py:234
  156.2 25.7 %collective-permute-start.23 = (bf16[4,128,640]{2,1,0:T(8,128)(2,1)S(1)}, bf16[4,128,640]{2,1,0:T(8,128)(2,1)}, u32[]{:S(2)}, u32[]{:S(2)}) collective-permute-start(bf16[4,128,640]{2,1,0:T(8,128)(2,1)S(1)} %get-tuple-element.24), channel_id=1, source_target_pairs={{0,24},{1,25},{2,26},{3,27},{4,28},{5,29},{6,30},{7,31},{8,0},{9,1... | collective-permute-start | bytes 1966088 | tf_op jit(solution)/shard_map/ppermute | solution.py:234
  158.2 16.2 %collective-permute-start.3 = (f32[2,8,128]{2,1,0:T(8,128)S(1)}, f32[2,8,128]{2,1,0:T(8,128)S(1)}, u32[]{:S(2)}, u32[]{:S(2)}) collective-permute-start(f32[2,8,128]{2,1,0:T(8,128)S(1)} %pad_maximum_fusion.3), channel_id=1, source_target_pairs={{0,256},{32,288},{64,320},{96,352},{128,384},{160,416},{192,448},{... | collective-permute-start | bytes 24584 | tf_op jit(solution)/shard_map/ppermute | solution.py:206
  168.0 15.6 %collective-permute-start.24 = (bf16[2,128,640]{2,1,0:T(8,128)(2,1)S(1)}, bf16[2,128,640]{2,1,0:T(8,128)(2,1)S(1)}, u32[]{:S(2)}, u32[]{:S(2)}) collective-permute-start(bf16[2,128,640]{2,1,0:T(8,128)(2,1)S(1)} %picks.18), channel_id=1, source_target_pairs={{0,16},{1,17},{2,18},{3,19},{4,20},{5,21},{6,22},{7,23},{8,24},{9,... | collective-permute-start | bytes 983048 | tf_op jit(solution)/shard_map/ppermute | solution.py:234
  (32 other events, 246.5 us)

commit v3 on v2

--- a/solution.py
+++ b/solution.py
@@ -32,38 +32,40 @@
 
 
 def payout_kernel(strike_ref, exit_ref, series_ref, out_ref):
-    b = pl.program_id(0)
     tau = lax.broadcasted_iota(jnp.int32, (BLK, DAY), 1)
     row = lax.broadcasted_iota(jnp.int32, (BLK, DAY), 0)
     upper = jnp.where(row <= tau, 1.0, 0.0).astype(jnp.bfloat16)
     tau = tau.astype(jnp.float32)
-
-    def column(ref):
-        line = ref[pl.ds(b, 1), :].astype(jnp.float32)
-        return jnp.transpose(jnp.broadcast_to(line, (BLK, BLK)))
-
-    start_on = tau >= column(strike_ref)
-    window_on = start_on & (tau < column(exit_ref))
-    for s in range(out_ref.shape[2] // DAY):
-        days = slice(s * DAY, (s + 1) * DAY)
-        x = series_ref[:, days].astype(jnp.float32)
-        masked = jnp.where(start_on, x, 0.0).astype(jnp.bfloat16)
-        running = jnp.dot(masked, upper, preferred_element_type=jnp.float32)
-        v = 0.3 * running + x
-        value = jnp.maximum(v, 0.0) + jnp.log1p(jnp.exp(-jnp.abs(v)))
-        out_ref[0, :, days] = jnp.where(window_on, value, 0.0).astype(jnp.bfloat16)
+    count = out_ref.shape[0]
+    for i in range(count):
+        b = pl.program_id(0) * count + i
+
+        def column(ref):
+            line = ref[pl.ds(b, 1), :].astype(jnp.float32)
+            return jnp.transpose(jnp.broadcast_to(line, (BLK, BLK)))
+
+        start_on = tau >= column(strike_ref)
+        window_on = start_on & (tau < column(exit_ref))
+        for s in range(out_ref.shape[2] // DAY):
+            days = slice(s * DAY, (s + 1) * DAY)
+            x = series_ref[i * BLK:(i + 1) * BLK, days].astype(jnp.float32)
+            masked = jnp.where(start_on, x, 0.0).astype(jnp.bfloat16)
+            running = jnp.dot(masked, upper, preferred_element_type=jnp.float32)
+            v = 0.3 * running + x
+            value = jnp.maximum(v, 0.0) + jnp.log1p(jnp.exp(-jnp.abs(v)))
+            out_ref[i, :, days] = jnp.where(window_on, value, 0.0).astype(jnp.bfloat16)
 
 
 def payouts(series, strike, leave):
     rows, days = series.shape
-    blocks = rows // BLK
+    blocks, count = rows // BLK, 4
     lines = pl.BlockSpec((blocks, BLK), lambda b: (0, 0))
     return pl.pallas_call(
         payout_kernel,
-        grid=(blocks,),
+        grid=(blocks // count,),
         out_shape=jax.ShapeDtypeStruct((blocks, BLK, days), jnp.bfloat16),
-        in_specs=[lines, lines, pl.BlockSpec((BLK, days), lambda b: (b, 0))],
-        out_specs=pl.BlockSpec((1, BLK, days), lambda b: (b, 0, 0)),
+        in_specs=[lines, lines, pl.BlockSpec((count * BLK, days), lambda b: (b, 0))],
+        out_specs=pl.BlockSpec((count, BLK, days), lambda b: (b, 0, 0)),
         name="payouts",
     )(strike.reshape(blocks, BLK), leave.reshape(blocks, BLK), series)
 
@@ -161,7 +163,7 @@
             keep_ref[target, p] = jnp.where(core == 0, near_rows, far_rows)
             send_ref[target, p] = jnp.where(core == 0, far_rows, near_rows)
 
-    pl.loop(0, pair_ref.shape[0], unroll=4)(one)
+    pl.loop(0, pair_ref.shape[0], unroll=8)(one)
 
 
 def grams(factor, table, place, pairs, farms, stations):

time: 247 us -> 242 us (0.980)
  Pallas kernels: 46.2 us -> 42.3 us
  waiting for transfers between devices: 38.9 us -> 41.6 us
    ppermute x4, starting transfers between devices: 17.7 us -> 9.45 us  [standardised(): other = lax.ppermute(state, 'season', hop)]
    ppermute x23, starting transfers between devices: 75.9 us -> 83 us  [shards(): along = lambda v, hop: lax.ppermute(v, 'farm', hop)]
    ppermute x23, waiting for transfers between devices: 24.2 us -> 29.1 us  [shards(): along = lambda v, hop: lax.ppermute(v, 'farm', hop)]
    ppermute x4, waiting for transfers between devices: 9.68 us -> 4.83 us  [standardised(): other = lax.ppermute(state, 'season', hop)]
    pallas_call x1, Pallas kernels: 6.89 us -> 4.23 us  [payouts(): pl.pallas_call(payout_kernel, grid=(blocks // count,), out_shape=jax.Shap...]
    all_to_all x1, waiting for transfers between devices: 0.71 us -> 3.37 us  [shards(): lax.all_to_all(jnp.broadcast_to(mine, (NY, mine.shape[1])), 'farm', 0, 0,...]
  transfers between devices with their start and end apart: 29 -> 29, of which waited for: 10 -> 13; matrix products, arithmetic and copies ran while one was open for 3% -> 3% of each run, Pallas kernels for 13% -> 13%
where the time goes in v3:
time: 242 us; the launch traced here: 241 us
  starting transfers between devices  101 us (42%)
  Pallas kernels  42.3 us (17%)
  waiting for transfers between devices  41.6 us (17%)
  blocking collectives  34.1 us (14%)
  local copies, waits for them, and re-layouts  13.7 us (6%)
  other arithmetic  7.03 us (3%)
    ppermute x23, starting transfers between devices, shards(): along = lambda v, hop: lax.ppermute(v, 'farm', hop)  83 us
    all_to_all x1, blocking collectives, season_sum(): lax.all_to_all(part.astype(jnp.float16), 'season', 0, 0, axis_index_group...  34.1 us
    ppermute x23, waiting for transfers between devices, shards(): along = lambda v, hop: lax.ppermute(v, 'farm', hop)  29.1 us
    pallas_call x10, Pallas kernels, picks(): pl.pallas_call(lambda *refs: pick_kernel(backs, steps, *refs), out_shape=...  26 us
    pallas_call x1, Pallas kernels, grams(): pl.pallas_call(lambda *refs: gram_kernel(factor, *refs), out_shape=[shape...  12 us
    ppermute x4, starting transfers between devices, standardised(): other = lax.ppermute(state, 'season', hop)  9.45 us
    unnamed x56, local copies, waits for them, and re-layouts  9.12 us
    all_to_all x1, starting transfers between devices, shards(): lax.all_to_all(jnp.broadcast_to(mine, (NY, mine.shape[1])), 'farm', 0, 0,...  7.1 us
  transfers between devices with their start and end apart: 29, of which 13 were waited for; matrix products, arithmetic and copies ran while one was open for 3% of the time, Pallas kernels for 13%

profile of v3, /device:TPU:6, one launch (start us, length us, event | category | flops | bytes accessed | tf_op | source)
XLA Modules:
  0.0 241.0 jit_solution(5852853837379870413)
XLA Ops:
  1.5 7.1 %all-to-all-start = ((s32[8,1,64]{2,1,0:T(1,128)}), s32[8,1,64]{2,1,0:T(1,128)S(1)}, u32[]{:S(2)}, u32[]{:S(2)}) async-start(s32[8,1,64]{2,1,0:T(1,128)} %broadcast_in_dim.9), calls=%async_computation | async-start | bytes 8192 | tf_op jit(solution)/shard_map/all_to_all | solution.py:238
  8.6 4.2 %payouts.1.refs_0_ = bf16[8,128,640]{2,1,0:T(8,128)(2,1)} custom-call(s32[8,128]{1,0:T(8,128)} %bitcast.109, s32[8,128]{1,0:T(8,128)} %bitcast.110, bf16[1024,640]{1,0:T(8,128)(2,1)} %series_ref.1), custom_call_target="tpu_custom_call" | custom-call | tf_op jit(solution)/shard_map/payouts/pallas_call | solution.py:63
  19.4 3.4 %collective-permute-start.4 = (bf16[8,128,640]{2,1,0:T(8,128)(2,1)}, bf16[8,128,640]{2,1,0:T(8,128)(2,1)S(1)}, u32[]{:S(2)}, u32[]{:S(2)}) collective-permute-start(bf16[8,128,640]{2,1,0:T(8,128)(2,1)} %pass_on.4.refs_2_.refs_4_), channel_id=1, source_target_pairs={{0,1},{1,2},{2,3},{3,4},{4,5},{5,6},{6,7},{7,0},{8,9},{9,10},{10,1... | collective-permute-start | bytes 3932168 | tf_op jit(solution)/shard_map/ppermute | solution.py:236
  35.4 4.0 %collective-permute-start.6 = (bf16[2,128,640]{2,1,0:T(8,128)(2,1)S(1)}, bf16[2,128,640]{2,1,0:T(8,128)(2,1)S(1)}, u32[]{:S(2)}, u32[]{:S(2)}) collective-permute-start(bf16[2,128,640]{2,1,0:T(8,128)(2,1)S(1)} %get-tuple-element.17), channel_id=1, source_target_pairs={{0,8},{1,9},{2,10},{3,11},{4,12},{5,13},{6,14},{7,15},{8,16},{9,17... | collective-permute-start | bytes 983048 | tf_op jit(solution)/shard_map/ppermute | solution.py:236
  41.4 6.8 %collective-permute-done.8.refs_3_.refs_6_ = bf16[8,128,640]{2,1,0:T(8,128)(2,1)} collective-permute-done((bf16[8,128,640]{2,1,0:T(8,128)(2,1)}, bf16[8,128,640]{2,1,0:T(8,128)(2,1)}, u32[]{:S(2)}, u32[]{:S(2)}) %collective-permute-start.8) | collective-permute-done | bytes 1310752 | tf_op jit(solution)/shard_map/ppermute | solution.py:236
  48.2 3.8 %collective-permute-start.12 = (bf16[8,128,640]{2,1,0:T(8,128)(2,1)}, bf16[8,128,640]{2,1,0:T(8,128)(2,1)}, u32[]{:S(2)}, u32[]{:S(2)}) collective-permute-start(bf16[8,128,640]{2,1,0:T(8,128)(2,1)} %collective-permute-done.8.refs_3_.refs_6_), channel_id=1, source_target_pairs={{0,7},{1,0},{2,1},{3,2},{4,3},{5,4},{6,5},{7,6},{8,15},{9,8},{10,9... | collective-permute-start | bytes 3932168 | tf_op jit(solution)/shard_map/ppermute | solution.py:236
  61.6 4.0 %collective-permute-start.10 = (bf16[4,128,640]{2,1,0:T(8,128)(2,1)S(1)}, bf16[4,128,640]{2,1,0:T(8,128)(2,1)S(1)}, u32[]{:S(2)}, u32[]{:S(2)}) collective-permute-start(bf16[4,128,640]{2,1,0:T(8,128)(2,1)S(1)} %get-tuple-element.19), channel_id=1, source_target_pairs={{0,8},{1,9},{2,10},{3,11},{4,12},{5,13},{6,14},{7,15},{8,16},{9,17... | collective-permute-start | bytes 1966088 | tf_op jit(solution)/shard_map/ppermute | solution.py:236
  70.5 8.1 %collective-permute-done.12.refs_3_.refs_8_ = bf16[8,128,640]{2,1,0:T(8,128)(2,1)} collective-permute-done((bf16[8,128,640]{2,1,0:T(8,128)(2,1)}, bf16[8,128,640]{2,1,0:T(8,128)(2,1)}, u32[]{:S(2)}, u32[]{:S(2)}) %collective-permute-start.12) | collective-permute-done | bytes 1310752 | tf_op jit(solution)/shard_map/ppermute | solution.py:236
  78.5 5.2 %collective-permute-start.16 = (bf16[8,128,640]{2,1,0:T(8,128)(2,1)}, bf16[8,128,640]{2,1,0:T(8,128)(2,1)S(1)}, u32[]{:S(2)}, u32[]{:S(2)}) collective-permute-start(bf16[8,128,640]{2,1,0:T(8,128)(2,1)} %collective-permute-done.12.refs_3_.refs_8_), channel_id=1, source_target_pairs={{0,7},{1,0},{2,1},{3,2},{4,3},{5,4},{6,5},{7,6},{8,15},{9,8},{10,9... | collective-permute-start | bytes 3932168 | tf_op jit(solution)/shard_map/ppermute | solution.py:236
  89.1 13.5 %collective-permute-start.13 = (bf16[8,128,640]{2,1,0:T(8,128)(2,1)}, bf16[8,128,640]{2,1,0:T(8,128)(2,1)S(1)}, u32[]{:S(2)}, u32[]{:S(2)}) collective-permute-start(bf16[8,128,640]{2,1,0:T(8,128)(2,1)} %pass_on.6.refs_2_.refs_7_), channel_id=1, source_target_pairs={{0,1},{1,2},{2,3},{3,4},{4,5},{5,6},{6,7},{7,0},{8,9},{9,10},{10,1... | collective-permute-start | bytes 3932168 | tf_op jit(solution)/shard_map/ppermute | solution.py:236
  104.5 4.8 %collective-permute-done.1.refs_5_ = f32[2,8,128]{2,1,0:T(8,128)S(1)} collective-permute-done((f32[2,8,128]{2,1,0:T(8,128)S(1)}, f32[2,8,128]{2,1,0:T(8,128)S(1)}, u32[]{:S(2)}, u32[]{:S(2)}) %collective-permute-start.1) | collective-permute-done | bytes 8224 | tf_op jit(solution)/shard_map/ppermute | solution.py:208
  115.0 3.4 %picks.15 = (bf16[4,128,640]{2,1,0:T(8,128)(2,1)}, bf16[4,128,640]{2,1,0:T(8,128)(2,1)}) custom-call(s32[8,64]{1,0:T(8,128)S(1)} %bitcast.100, s32[4]{0:T(128)S(1)} %pad_add_fusion.refs_1_, bf16[8,128,640]{2,1,0:T(8,128)(2,1)S(1)} %copy-done.4, bf16[8,128,640]{2,1,0:T(8,128)(2,1)} %collective-permute-done.12.refs_3_.refs_8_, ...), custom_call_target="tpu_custom_call" | custom-call | bytes 2621440 | tf_op jit(solution)/shard_map/picks/pallas_call | solution.py:108
  120.4 3.9 %collective-permute-start.20 = (bf16[4,128,640]{2,1,0:T(8,128)(2,1)}, bf16[4,128,640]{2,1,0:T(8,128)(2,1)}, u32[]{:S(2)}, u32[]{:S(2)}) collective-permute-start(bf16[4,128,640]{2,1,0:T(8,128)(2,1)} %get-tuple-element.22), channel_id=1, source_target_pairs={{0,24},{1,25},{2,26},{3,27},{4,28},{5,29},{6,30},{7,31},{8,0},{9,1... | collective-permute-start | bytes 1966088 | tf_op jit(solution)/shard_map/ppermute | solution.py:236
  125.4 4.0 %collective-permute-start.18 = (bf16[8,64,640]{2,1,0:T(8,128)(2,1)}, bf16[8,64,640]{2,1,0:T(8,128)(2,1)}, u32[]{:S(2)}, u32[]{:S(2)}) collective-permute-start(bf16[8,64,640]{2,1,0:T(8,128)(2,1)} %slice.53), channel_id=1, source_target_pairs={{0,7},{1,0},{2,1},{3,2},{4,3},{5,4},{6,5},{7,6},{8,15},{9,8},{10,9... | collective-permute-start | bytes 1966088 | tf_op jit(solution)/shard_map/ppermute | solution.py:236
  129.4 3.4 %collective-permute-done.15.refs_1_.refs_4_.refs_19_ = bf16[4,128,640]{2,1,0:T(8,128)(2,1)S(1)} collective-permute-done((bf16[4,128,640]{2,1,0:T(8,128)(2,1)S(1)}, bf16[4,128,640]{2,1,0:T(8,128)(2,1)S(1)}, u32[]{:S(2)}, u32[]{:S(2)}) %collective-permute-start.15) | collective-permute-done | bytes 655392 | tf_op jit(solution)/shard_map/ppermute | solution.py:236
  137.9 3.8 %collective-permute-start.17 = (bf16[8,64,640]{2,1,0:T(8,128)(2,1)}, bf16[8,64,640]{2,1,0:T(8,128)(2,1)S(1)}, u32[]{:S(2)}, u32[]{:S(2)}) collective-permute-start(bf16[8,64,640]{2,1,0:T(8,128)(2,1)} %slice.52), channel_id=1, source_target_pairs={{0,1},{1,2},{2,3},{3,4},{4,5},{5,6},{6,7},{7,0},{8,9},{9,10},{10,1... | collective-permute-start | bytes 1966088 | tf_op jit(solution)/shard_map/ppermute | solution.py:236
  154.2 3.9 %collective-permute-start.23 = (bf16[4,128,640]{2,1,0:T(8,128)(2,1)S(1)}, bf16[4,128,640]{2,1,0:T(8,128)(2,1)}, u32[]{:S(2)}, u32[]{:S(2)}) collective-permute-start(bf16[4,128,640]{2,1,0:T(8,128)(2,1)S(1)} %get-tuple-element.24), channel_id=1, source_target_pairs={{0,24},{1,25},{2,26},{3,27},{4,28},{5,29},{6,30},{7,31},{8,0},{9,1... | collective-permute-start | bytes 1966088 | tf_op jit(solution)/shard_map/ppermute | solution.py:236
  158.2 3.7 %collective-permute-start.3 = (f32[2,8,128]{2,1,0:T(8,128)S(1)}, f32[2,8,128]{2,1,0:T(8,128)S(1)}, u32[]{:S(2)}, u32[]{:S(2)}) collective-permute-start(f32[2,8,128]{2,1,0:T(8,128)S(1)} %pad_maximum_fusion.3), channel_id=1, source_target_pairs={{0,256},{32,288},{64,320},{96,352},{128,384},{160,416},{192,448},{... | collective-permute-start | bytes 24584 | tf_op jit(solution)/shard_map/ppermute | solution.py:208
  164.0 3.4 %collective-permute-start.24 = (bf16[2,128,640]{2,1,0:T(8,128)(2,1)S(1)}, bf16[2,128,640]{2,1,0:T(8,128)(2,1)S(1)}, u32[]{:S(2)}, u32[]{:S(2)}) collective-permute-start(bf16[2,128,640]{2,1,0:T(8,128)(2,1)S(1)} %picks.18), channel_id=1, source_target_pairs={{0,16},{1,17},{2,18},{3,19},{4,20},{5,21},{6,22},{7,23},{8,24},{9,... | collective-permute-start | bytes 983048 | tf_op jit(solution)/shard_map/ppermute | solution.py:236
  169.9 3.6 %collective-permute-start.25 = (bf16[2,128,640]{2,1,0:T(8,128)(2,1)S(1)}, bf16[2,128,640]{2,1,0:T(8,128)(2,1)S(1)}, u32[]{:S(2)}, u32[]{:S(2)}) collective-permute-start(bf16[2,128,640]{2,1,0:T(8,128)(2,1)S(1)} %get-tuple-element.25), channel_id=1, source_target_pairs={{0,8},{1,9},{2,10},{3,11},{4,12},{5,13},{6,14},{7,15},{8,16},{9,17... | collective-permute-start | bytes 983048 | tf_op jit(solution)/shard_map/ppermute | solution.py:236
  178.7 3.7 %collective-permute-done.24.refs_25_ = bf16[2,128,640]{2,1,0:T(8,128)(2,1)S(1)} collective-permute-done((bf16[2,128,640]{2,1,0:T(8,128)(2,1)S(1)}, bf16[2,128,640]{2,1,0:T(8,128)(2,1)S(1)}, u32[]{:S(2)}, u32[]{:S(2)}) %collective-permute-start.24) | collective-permute-done | bytes 327712 | tf_op jit(solution)/shard_map/ppermute | solution.py:236
  185.9 12.0 %grams.1 = (f32[8,64,8,128]{3,2,1,0:T(8,128)}, f32[8,64,8,128]{3,2,1,0:T(8,128)}) custom-call(s32[8,64]{1,0:T(8,128)S(1)} %bitcast.105, s32[4]{0:T(128)S(1)} %pad_add_fusion.refs_1_, s32[64,2]{1,0:T(8,128)S(1)} %copy.19.refs_2_, bf16[8,128,640]{2,1,0:T(8,128)(2,1)} %bitcast.106, bf16[8,128,640]{2,1,0:T(8,128)(2,1)} %pass_on.4.refs_2_.refs_4_, ...), custom_call_target="tpu_custom_call" | custom-call | flops 1342177280 | bytes 10485760 | tf_op jit(solution)/shard_map/grams/pallas_call | solution.py:174
  199.8 4.3 %collective-permute-done.27 = f32[8,64,8,128]{3,2,1,0:T(8,128)S(1)} collective-permute-done((f32[8,64,8,128]{3,2,1,0:T(8,128)}, f32[8,64,8,128]{3,2,1,0:T(8,128)S(1)}, u32[]{:S(2)}, u32[]{:S(2)}) %collective-permute-start.27) | collective-permute-done | bytes 2097184 | tf_op jit(solution)/shard_map/ppermute | solution.py:223
  206.0 34.1 %all_to_all.13 = f16[8,64,8,128]{3,2,1,0:T(8,128)(2,1)S(1)} all-to-all(f16[8,64,8,128]{3,2,1,0:T(8,128)(2,1)S(1)} %add_convert_fusion), channel_id=1, replica_groups={{0,64,128,192,256,320,384,448},{32,96,160,224,288,352,416,480},{1,65,12..., dimensions={0} | all-to-all | bytes 2097152 | tf_op jit(solution)/shard_map/all_to_all | solution.py:225
  (128 shorter events, 87.8 us)
Async XLA Ops:
  1.5 14.7 %all-to-all-start = ((s32[8,1,64]{2,1,0:T(1,128)}), s32[8,1,64]{2,1,0:T(1,128)S(1)}, u32[]{:S(2)}, u32[]{:S(2)}) async-start(s32[8,1,64]{2,1,0:T(1,128)} %broadcast_in_dim.9), calls=%async_computation | async-start | bytes 8192 | tf_op jit(solution)/shard_map/all_to_all | solution.py:238
  16.8 31.4 %collective-permute-start.8 = (bf16[8,128,640]{2,1,0:T(8,128)(2,1)}, bf16[8,128,640]{2,1,0:T(8,128)(2,1)}, u32[]{:S(2)}, u32[]{:S(2)}) collective-permute-start(bf16[8,128,640]{2,1,0:T(8,128)(2,1)} %pass_on.4.refs_2_.refs_4_), channel_id=1, source_target_pairs={{0,7},{1,0},{2,1},{3,2},{4,3},{5,4},{6,5},{7,6},{8,15},{9,8},{10,9... | collective-permute-start | bytes 3932168 | tf_op jit(solution)/shard_map/ppermute | solution.py:236
  19.4 33.3 %collective-permute-start.4 = (bf16[8,128,640]{2,1,0:T(8,128)(2,1)}, bf16[8,128,640]{2,1,0:T(8,128)(2,1)S(1)}, u32[]{:S(2)}, u32[]{:S(2)}) collective-permute-start(bf16[8,128,640]{2,1,0:T(8,128)(2,1)} %pass_on.4.refs_2_.refs_4_), channel_id=1, source_target_pairs={{0,1},{1,2},{2,3},{3,4},{4,5},{5,6},{6,7},{7,0},{8,9},{9,10},{10,1... | collective-permute-start | bytes 3932168 | tf_op jit(solution)/shard_map/ppermute | solution.py:236
  26.2 13.3 %collective-permute-start = (f32[2,8,128]{2,1,0:T(8,128)S(1)}, f32[2,8,128]{2,1,0:T(8,128)S(1)}, u32[]{:S(2)}, u32[]{:S(2)}) collective-permute-start(f32[2,8,128]{2,1,0:T(8,128)S(1)} %pad_maximum_fusion), channel_id=1, source_target_pairs={{0,32},{32,0},{64,96},{96,64},{128,160},{160,128},{192,224},{224,1... | collective-permute-start | bytes 24584 | tf_op jit(solution)/shard_map/ppermute | solution.py:208
  32.1 19.9 %collective-permute-start.5 = (bf16[2,128,640]{2,1,0:T(8,128)(2,1)S(1)}, bf16[2,128,640]{2,1,0:T(8,128)(2,1)S(1)}, u32[]{:S(2)}, u32[]{:S(2)}) collective-permute-start(bf16[2,128,640]{2,1,0:T(8,128)(2,1)S(1)} %picks.10), channel_id=1, source_target_pairs={{0,16},{1,17},{2,18},{3,19},{4,20},{5,21},{6,22},{7,23},{8,24},{9,... | collective-permute-start | bytes 983048 | tf_op jit(solution)/shard_map/ppermute | solution.py:236
  35.4 16.6 %collective-permute-start.6 = (bf16[2,128,640]{2,1,0:T(8,128)(2,1)S(1)}, bf16[2,128,640]{2,1,0:T(8,128)(2,1)S(1)}, u32[]{:S(2)}, u32[]{:S(2)}) collective-permute-start(bf16[2,128,640]{2,1,0:T(8,128)(2,1)S(1)} %get-tuple-element.17), channel_id=1, source_target_pairs={{0,8},{1,9},{2,10},{3,11},{4,12},{5,13},{6,14},{7,15},{8,16},{9,17... | collective-permute-start | bytes 983048 | tf_op jit(solution)/shard_map/ppermute | solution.py:236
  39.5 13.2 %collective-permute-start.7 = (bf16[2,128,640]{2,1,0:T(8,128)(2,1)S(1)}, bf16[2,128,640]{2,1,0:T(8,128)(2,1)S(1)}, u32[]{:S(2)}, u32[]{:S(2)}) collective-permute-start(bf16[2,128,640]{2,1,0:T(8,128)(2,1)S(1)} %get-tuple-element.18), channel_id=1, source_target_pairs={{0,24},{1,25},{2,26},{3,27},{4,28},{5,29},{6,30},{7,31},{8,0},{9,1... | collective-permute-start | bytes 983048 | tf_op jit(solution)/shard_map/ppermute | solution.py:236
  48.2 30.4 %collective-permute-start.12 = (bf16[8,128,640]{2,1,0:T(8,128)(2,1)}, bf16[8,128,640]{2,1,0:T(8,128)(2,1)}, u32[]{:S(2)}, u32[]{:S(2)}) collective-permute-start(bf16[8,128,640]{2,1,0:T(8,128)(2,1)} %collective-permute-done.8.refs_3_.refs_6_), channel_id=1, source_target_pairs={{0,7},{1,0},{2,1},{3,2},{4,3},{5,4},{6,5},{7,6},{8,15},{9,8},{10,9... | collective-permute-start | bytes 3932168 | tf_op jit(solution)/shard_map/ppermute | solution.py:236
  54.4 33.6 %collective-permute-start.9 = (bf16[8,128,640]{2,1,0:T(8,128)(2,1)}, bf16[8,128,640]{2,1,0:T(8,128)(2,1)S(1)}, u32[]{:S(2)}, u32[]{:S(2)}) collective-permute-start(bf16[8,128,640]{2,1,0:T(8,128)(2,1)} %pass_on.5.refs_2_.refs_5_), channel_id=1, source_target_pairs={{0,1},{1,2},{2,3},{3,4},{4,5},{5,6},{6,7},{7,0},{8,9},{9,10},{10,1... | collective-permute-start | bytes 3932168 | tf_op jit(solution)/shard_map/ppermute | solution.py:236
  61.6 25.5 %collective-permute-start.10 = (bf16[4,128,640]{2,1,0:T(8,128)(2,1)S(1)}, bf16[4,128,640]{2,1,0:T(8,128)(2,1)S(1)}, u32[]{:S(2)}, u32[]{:S(2)}) collective-permute-start(bf16[4,128,640]{2,1,0:T(8,128)(2,1)S(1)} %get-tuple-element.19), channel_id=1, source_target_pairs={{0,8},{1,9},{2,10},{3,11},{4,12},{5,13},{6,14},{7,15},{8,16},{9,17... | collective-permute-start | bytes 1966088 | tf_op jit(solution)/shard_map/ppermute | solution.py:236
  65.6 21.5 %collective-permute-start.11 = (bf16[4,128,640]{2,1,0:T(8,128)(2,1)S(1)}, bf16[4,128,640]{2,1,0:T(8,128)(2,1)}, u32[]{:S(2)}, u32[]{:S(2)}) collective-permute-start(bf16[4,128,640]{2,1,0:T(8,128)(2,1)S(1)} %get-tuple-element.20), channel_id=1, source_target_pairs={{0,24},{1,25},{2,26},{3,27},{4,28},{5,29},{6,30},{7,31},{8,0},{9,1... | collective-permute-start | bytes 1966088 | tf_op jit(solution)/shard_map/ppermute | solution.py:236
  78.5 45.8 %collective-permute-start.16 = (bf16[8,128,640]{2,1,0:T(8,128)(2,1)}, bf16[8,128,640]{2,1,0:T(8,128)(2,1)S(1)}, u32[]{:S(2)}, u32[]{:S(2)}) collective-permute-start(bf16[8,128,640]{2,1,0:T(8,128)(2,1)} %collective-permute-done.12.refs_3_.refs_8_), channel_id=1, source_target_pairs={{0,7},{1,0},{2,1},{3,2},{4,3},{5,4},{6,5},{7,6},{8,15},{9,8},{10,9... | collective-permute-start | bytes 3932168 | tf_op jit(solution)/shard_map/ppermute | solution.py:236
  83.8 25.6 %collective-permute-start.14 = (bf16[4,128,640]{2,1,0:T(8,128)(2,1)}, bf16[4,128,640]{2,1,0:T(8,128)(2,1)}, u32[]{:S(2)}, u32[]{:S(2)}) collective-permute-start(bf16[4,128,640]{2,1,0:T(8,128)(2,1)} %picks.13), channel_id=1, source_target_pairs={{0,16},{1,17},{2,18},{3,19},{4,20},{5,21},{6,22},{7,23},{8,24},{9,... | collective-permute-start | bytes 1966088 | tf_op jit(solution)/shard_map/ppermute | solution.py:236
  89.1 45.7 %collective-permute-start.13 = (bf16[8,128,640]{2,1,0:T(8,128)(2,1)}, bf16[8,128,640]{2,1,0:T(8,128)(2,1)S(1)}, u32[]{:S(2)}, u32[]{:S(2)}) collective-permute-start(bf16[8,128,640]{2,1,0:T(8,128)(2,1)} %pass_on.6.refs_2_.refs_7_), channel_id=1, source_target_pairs={{0,1},{1,2},{2,3},{3,4},{4,5},{5,6},{6,7},{7,0},{8,9},{9,10},{10,1... | collective-permute-start | bytes 3932168 | tf_op jit(solution)/shard_map/ppermute | solution.py:236
  113.1 19.7 %collective-permute-start.15 = (bf16[4,128,640]{2,1,0:T(8,128)(2,1)S(1)}, bf16[4,128,640]{2,1,0:T(8,128)(2,1)S(1)}, u32[]{:S(2)}, u32[]{:S(2)}) collective-permute-start(bf16[4,128,640]{2,1,0:T(8,128)(2,1)S(1)} %picks.14), channel_id=1, source_target_pairs={{0,16},{1,17},{2,18},{3,19},{4,20},{5,21},{6,22},{7,23},{8,24},{9,... | collective-permute-start | bytes 1966088 | tf_op jit(solution)/shard_map/ppermute | solution.py:236
  118.5 29.0 %collective-permute-start.19 = (bf16[4,128,640]{2,1,0:T(8,128)(2,1)}, bf16[4,128,640]{2,1,0:T(8,128)(2,1)}, u32[]{:S(2)}, u32[]{:S(2)}) collective-permute-start(bf16[4,128,640]{2,1,0:T(8,128)(2,1)} %get-tuple-element.21), channel_id=1, source_target_pairs={{0,8},{1,9},{2,10},{3,11},{4,12},{5,13},{6,14},{7,15},{8,16},{9,17... | collective-permute-start | bytes 1966088 | tf_op jit(solution)/shard_map/ppermute | solution.py:236
  120.4 28.6 %collective-permute-start.20 = (bf16[4,128,640]{2,1,0:T(8,128)(2,1)}, bf16[4,128,640]{2,1,0:T(8,128)(2,1)}, u32[]{:S(2)}, u32[]{:S(2)}) collective-permute-start(bf16[4,128,640]{2,1,0:T(8,128)(2,1)} %get-tuple-element.22), channel_id=1, source_target_pairs={{0,24},{1,25},{2,26},{3,27},{4,28},{5,29},{6,30},{7,31},{8,0},{9,1... | collective-permute-start | bytes 1966088 | tf_op jit(solution)/shard_map/ppermute | solution.py:236
  125.4 32.8 %collective-permute-start.18 = (bf16[8,64,640]{2,1,0:T(8,128)(2,1)}, bf16[8,64,640]{2,1,0:T(8,128)(2,1)}, u32[]{:S(2)}, u32[]{:S(2)}) collective-permute-start(bf16[8,64,640]{2,1,0:T(8,128)(2,1)} %slice.53), channel_id=1, source_target_pairs={{0,7},{1,0},{2,1},{3,2},{4,3},{5,4},{6,5},{7,6},{8,15},{9,8},{10,9... | collective-permute-start | bytes 1966088 | tf_op jit(solution)/shard_map/ppermute | solution.py:236
  137.9 24.1 %collective-permute-start.17 = (bf16[8,64,640]{2,1,0:T(8,128)(2,1)}, bf16[8,64,640]{2,1,0:T(8,128)(2,1)S(1)}, u32[]{:S(2)}, u32[]{:S(2)}) collective-permute-start(bf16[8,64,640]{2,1,0:T(8,128)(2,1)} %slice.52), channel_id=1, source_target_pairs={{0,1},{1,2},{2,3},{3,4},{4,5},{5,6},{6,7},{7,0},{8,9},{9,10},{10,1... | collective-permute-start | bytes 1966088 | tf_op jit(solution)/shard_map/ppermute | solution.py:236
  145.3 28.3 %collective-permute-start.21 = (bf16[4,128,640]{2,1,0:T(8,128)(2,1)S(1)}, bf16[4,128,640]{2,1,0:T(8,128)(2,1)}, u32[]{:S(2)}, u32[]{:S(2)}) collective-permute-start(bf16[4,128,640]{2,1,0:T(8,128)(2,1)S(1)} %picks.16), channel_id=1, source_target_pairs={{0,16},{1,17},{2,18},{3,19},{4,20},{5,21},{6,22},{7,23},{8,24},{9,... | collective-permute-start | bytes 1966088 | tf_op jit(solution)/shard_map/ppermute | solution.py:236
  152.3 25.6 %collective-permute-start.22 = (bf16[4,128,640]{2,1,0:T(8,128)(2,1)}, bf16[4,128,640]{2,1,0:T(8,128)(2,1)S(1)}, u32[]{:S(2)}, u32[]{:S(2)}) collective-permute-start(bf16[4,128,640]{2,1,0:T(8,128)(2,1)} %get-tuple-element.23), channel_id=1, source_target_pairs={{0,8},{1,9},{2,10},{3,11},{4,12},{5,13},{6,14},{7,15},{8,16},{9,17... | collective-permute-start | bytes 1966088 | tf_op jit(solution)/shard_map/ppermute | solution.py:236
  154.2 24.5 %collective-permute-start.23 = (bf16[4,128,640]{2,1,0:T(8,128)(2,1)S(1)}, bf16[4,128,640]{2,1,0:T(8,128)(2,1)}, u32[]{:S(2)}, u32[]{:S(2)}) collective-permute-start(bf16[4,128,640]{2,1,0:T(8,128)(2,1)S(1)} %get-tuple-element.24), channel_id=1, source_target_pairs={{0,24},{1,25},{2,26},{3,27},{4,28},{5,29},{6,30},{7,31},{8,0},{9,1... | collective-permute-start | bytes 1966088 | tf_op jit(solution)/shard_map/ppermute | solution.py:236
  164.0 18.4 %collective-permute-start.24 = (bf16[2,128,640]{2,1,0:T(8,128)(2,1)S(1)}, bf16[2,128,640]{2,1,0:T(8,128)(2,1)S(1)}, u32[]{:S(2)}, u32[]{:S(2)}) collective-permute-start(bf16[2,128,640]{2,1,0:T(8,128)(2,1)S(1)} %picks.18), channel_id=1, source_target_pairs={{0,16},{1,17},{2,18},{3,19},{4,20},{5,21},{6,22},{7,23},{8,24},{9,... | collective-permute-start | bytes 983048 | tf_op jit(solution)/shard_map/ppermute | solution.py:236
  169.9 13.5 %collective-permute-start.25 = (bf16[2,128,640]{2,1,0:T(8,128)(2,1)S(1)}, bf16[2,128,640]{2,1,0:T(8,128)(2,1)S(1)}, u32[]{:S(2)}, u32[]{:S(2)}) collective-permute-start(bf16[2,128,640]{2,1,0:T(8,128)(2,1)S(1)} %get-tuple-element.25), channel_id=1, source_target_pairs={{0,8},{1,9},{2,10},{3,11},{4,12},{5,13},{6,14},{7,15},{8,16},{9,17... | collective-permute-start | bytes 983048 | tf_op jit(solution)/shard_map/ppermute | solution.py:236
  (32 other events, 253.7 us)

commit v4 on v3

--- a/solution.py
+++ b/solution.py
@@ -163,7 +163,7 @@
             keep_ref[target, p] = jnp.where(core == 0, near_rows, far_rows)
             send_ref[target, p] = jnp.where(core == 0, far_rows, near_rows)
 
-    pl.loop(0, pair_ref.shape[0], unroll=8)(one)
+    pl.loop(0, pair_ref.shape[0], unroll=16)(one)
 
 
 def grams(factor, table, place, pairs, farms, stations):

time: 242 us -> 242 us (level)
  no operation moved by 1% of the time
where the time goes in v4:
time: 242 us; the launch traced here: 240 us
  starting transfers between devices  101 us (42%)
  Pallas kernels  41.6 us (17%)
  waiting for transfers between devices  41.6 us (17%)
  blocking collectives  34.1 us (14%)
  local copies, waits for them, and re-layouts  13.7 us (6%)
  other arithmetic  7.03 us (3%)
    ppermute x23, starting transfers between devices, shards(): along = lambda v, hop: lax.ppermute(v, 'farm', hop)  83 us
    all_to_all x1, blocking collectives, season_sum(): lax.all_to_all(part.astype(jnp.float16), 'season', 0, 0, axis_index_group...  34.1 us
    ppermute x23, waiting for transfers between devices, shards(): along = lambda v, hop: lax.ppermute(v, 'farm', hop)  29.1 us
    pallas_call x10, Pallas kernels, picks(): pl.pallas_call(lambda *refs: pick_kernel(backs, steps, *refs), out_shape=...  26 us
    pallas_call x1, Pallas kernels, grams(): pl.pallas_call(lambda *refs: gram_kernel(factor, *refs), out_shape=[shape...  11.4 us
    ppermute x4, starting transfers between devices, standardised(): other = lax.ppermute(state, 'season', hop)  9.45 us
    unnamed x56, local copies, waits for them, and re-layouts  9.12 us
    all_to_all x1, starting transfers between devices, shards(): lax.all_to_all(jnp.broadcast_to(mine, (NY, mine.shape[1])), 'farm', 0, 0,...  7.1 us
  transfers between devices with their start and end apart: 29, of which 13 were waited for; matrix products, arithmetic and copies ran while one was open for 3% of the time, Pallas kernels for 13%

profile of v4, /device:TPU:6, one launch (start us, length us, event | category | flops | bytes accessed | tf_op | source)
XLA Modules:
  0.0 240.3 jit_solution(13880196004122470348)
XLA Ops:
  1.5 7.1 %all-to-all-start = ((s32[8,1,64]{2,1,0:T(1,128)}), s32[8,1,64]{2,1,0:T(1,128)S(1)}, u32[]{:S(2)}, u32[]{:S(2)}) async-start(s32[8,1,64]{2,1,0:T(1,128)} %broadcast_in_dim.9), calls=%async_computation | async-start | bytes 8192 | tf_op jit(solution)/shard_map/all_to_all | solution.py:238
  8.6 4.2 %payouts.1.refs_0_ = bf16[8,128,640]{2,1,0:T(8,128)(2,1)} custom-call(s32[8,128]{1,0:T(8,128)} %bitcast.109, s32[8,128]{1,0:T(8,128)} %bitcast.110, bf16[1024,640]{1,0:T(8,128)(2,1)} %series_ref.1), custom_call_target="tpu_custom_call" | custom-call | tf_op jit(solution)/shard_map/payouts/pallas_call | solution.py:63
  19.4 3.4 %collective-permute-start.4 = (bf16[8,128,640]{2,1,0:T(8,128)(2,1)}, bf16[8,128,640]{2,1,0:T(8,128)(2,1)S(1)}, u32[]{:S(2)}, u32[]{:S(2)}) collective-permute-start(bf16[8,128,640]{2,1,0:T(8,128)(2,1)} %pass_on.4.refs_2_.refs_4_), channel_id=1, source_target_pairs={{0,1},{1,2},{2,3},{3,4},{4,5},{5,6},{6,7},{7,0},{8,9},{9,10},{10,1... | collective-permute-start | bytes 3932168 | tf_op jit(solution)/shard_map/ppermute | solution.py:236
  35.4 4.0 %collective-permute-start.6 = (bf16[2,128,640]{2,1,0:T(8,128)(2,1)S(1)}, bf16[2,128,640]{2,1,0:T(8,128)(2,1)S(1)}, u32[]{:S(2)}, u32[]{:S(2)}) collective-permute-start(bf16[2,128,640]{2,1,0:T(8,128)(2,1)S(1)} %get-tuple-element.17), channel_id=1, source_target_pairs={{0,8},{1,9},{2,10},{3,11},{4,12},{5,13},{6,14},{7,15},{8,16},{9,17... | collective-permute-start | bytes 983048 | tf_op jit(solution)/shard_map/ppermute | solution.py:236
  41.4 6.8 %collective-permute-done.8.refs_3_.refs_6_ = bf16[8,128,640]{2,1,0:T(8,128)(2,1)} collective-permute-done((bf16[8,128,640]{2,1,0:T(8,128)(2,1)}, bf16[8,128,640]{2,1,0:T(8,128)(2,1)}, u32[]{:S(2)}, u32[]{:S(2)}) %collective-permute-start.8) | collective-permute-done | bytes 1310752 | tf_op jit(solution)/shard_map/ppermute | solution.py:236
  48.2 3.8 %collective-permute-start.12 = (bf16[8,128,640]{2,1,0:T(8,128)(2,1)}, bf16[8,128,640]{2,1,0:T(8,128)(2,1)}, u32[]{:S(2)}, u32[]{:S(2)}) collective-permute-start(bf16[8,128,640]{2,1,0:T(8,128)(2,1)} %collective-permute-done.8.refs_3_.refs_6_), channel_id=1, source_target_pairs={{0,7},{1,0},{2,1},{3,2},{4,3},{5,4},{6,5},{7,6},{8,15},{9,8},{10,9... | collective-permute-start | bytes 3932168 | tf_op jit(solution)/shard_map/ppermute | solution.py:236
  61.6 4.0 %collective-permute-start.10 = (bf16[4,128,640]{2,1,0:T(8,128)(2,1)S(1)}, bf16[4,128,640]{2,1,0:T(8,128)(2,1)S(1)}, u32[]{:S(2)}, u32[]{:S(2)}) collective-permute-start(bf16[4,128,640]{2,1,0:T(8,128)(2,1)S(1)} %get-tuple-element.19), channel_id=1, source_target_pairs={{0,8},{1,9},{2,10},{3,11},{4,12},{5,13},{6,14},{7,15},{8,16},{9,17... | collective-permute-start | bytes 1966088 | tf_op jit(solution)/shard_map/ppermute | solution.py:236
  70.5 8.1 %collective-permute-done.12.refs_3_.refs_8_ = bf16[8,128,640]{2,1,0:T(8,128)(2,1)} collective-permute-done((bf16[8,128,640]{2,1,0:T(8,128)(2,1)}, bf16[8,128,640]{2,1,0:T(8,128)(2,1)}, u32[]{:S(2)}, u32[]{:S(2)}) %collective-permute-start.12) | collective-permute-done | bytes 1310752 | tf_op jit(solution)/shard_map/ppermute | solution.py:236
  78.5 5.2 %collective-permute-start.16 = (bf16[8,128,640]{2,1,0:T(8,128)(2,1)}, bf16[8,128,640]{2,1,0:T(8,128)(2,1)S(1)}, u32[]{:S(2)}, u32[]{:S(2)}) collective-permute-start(bf16[8,128,640]{2,1,0:T(8,128)(2,1)} %collective-permute-done.12.refs_3_.refs_8_), channel_id=1, source_target_pairs={{0,7},{1,0},{2,1},{3,2},{4,3},{5,4},{6,5},{7,6},{8,15},{9,8},{10,9... | collective-permute-start | bytes 3932168 | tf_op jit(solution)/shard_map/ppermute | solution.py:236
  89.1 13.5 %collective-permute-start.13 = (bf16[8,128,640]{2,1,0:T(8,128)(2,1)}, bf16[8,128,640]{2,1,0:T(8,128)(2,1)S(1)}, u32[]{:S(2)}, u32[]{:S(2)}) collective-permute-start(bf16[8,128,640]{2,1,0:T(8,128)(2,1)} %pass_on.6.refs_2_.refs_7_), channel_id=1, source_target_pairs={{0,1},{1,2},{2,3},{3,4},{4,5},{5,6},{6,7},{7,0},{8,9},{9,10},{10,1... | collective-permute-start | bytes 3932168 | tf_op jit(solution)/shard_map/ppermute | solution.py:236
  104.5 4.8 %collective-permute-done.1.refs_5_ = f32[2,8,128]{2,1,0:T(8,128)S(1)} collective-permute-done((f32[2,8,128]{2,1,0:T(8,128)S(1)}, f32[2,8,128]{2,1,0:T(8,128)S(1)}, u32[]{:S(2)}, u32[]{:S(2)}) %collective-permute-start.1) | collective-permute-done | bytes 8224 | tf_op jit(solution)/shard_map/ppermute | solution.py:208
  115.0 3.4 %picks.15 = (bf16[4,128,640]{2,1,0:T(8,128)(2,1)}, bf16[4,128,640]{2,1,0:T(8,128)(2,1)}) custom-call(s32[8,64]{1,0:T(8,128)S(1)} %bitcast.100, s32[4]{0:T(128)S(1)} %pad_add_fusion.refs_1_, bf16[8,128,640]{2,1,0:T(8,128)(2,1)S(1)} %copy-done.4, bf16[8,128,640]{2,1,0:T(8,128)(2,1)} %collective-permute-done.12.refs_3_.refs_8_, ...), custom_call_target="tpu_custom_call" | custom-call | bytes 2621440 | tf_op jit(solution)/shard_map/picks/pallas_call | solution.py:108
  120.4 3.9 %collective-permute-start.20 = (bf16[4,128,640]{2,1,0:T(8,128)(2,1)}, bf16[4,128,640]{2,1,0:T(8,128)(2,1)}, u32[]{:S(2)}, u32[]{:S(2)}) collective-permute-start(bf16[4,128,640]{2,1,0:T(8,128)(2,1)} %get-tuple-element.22), channel_id=1, source_target_pairs={{0,24},{1,25},{2,26},{3,27},{4,28},{5,29},{6,30},{7,31},{8,0},{9,1... | collective-permute-start | bytes 1966088 | tf_op jit(solution)/shard_map/ppermute | solution.py:236
  125.4 4.0 %collective-permute-start.18 = (bf16[8,64,640]{2,1,0:T(8,128)(2,1)}, bf16[8,64,640]{2,1,0:T(8,128)(2,1)}, u32[]{:S(2)}, u32[]{:S(2)}) collective-permute-start(bf16[8,64,640]{2,1,0:T(8,128)(2,1)} %slice.53), channel_id=1, source_target_pairs={{0,7},{1,0},{2,1},{3,2},{4,3},{5,4},{6,5},{7,6},{8,15},{9,8},{10,9... | collective-permute-start | bytes 1966088 | tf_op jit(solution)/shard_map/ppermute | solution.py:236
  129.4 3.4 %collective-permute-done.15.refs_1_.refs_4_.refs_19_ = bf16[4,128,640]{2,1,0:T(8,128)(2,1)S(1)} collective-permute-done((bf16[4,128,640]{2,1,0:T(8,128)(2,1)S(1)}, bf16[4,128,640]{2,1,0:T(8,128)(2,1)S(1)}, u32[]{:S(2)}, u32[]{:S(2)}) %collective-permute-start.15) | collective-permute-done | bytes 655392 | tf_op jit(solution)/shard_map/ppermute | solution.py:236
  137.9 3.8 %collective-permute-start.17 = (bf16[8,64,640]{2,1,0:T(8,128)(2,1)}, bf16[8,64,640]{2,1,0:T(8,128)(2,1)S(1)}, u32[]{:S(2)}, u32[]{:S(2)}) collective-permute-start(bf16[8,64,640]{2,1,0:T(8,128)(2,1)} %slice.52), channel_id=1, source_target_pairs={{0,1},{1,2},{2,3},{3,4},{4,5},{5,6},{6,7},{7,0},{8,9},{9,10},{10,1... | collective-permute-start | bytes 1966088 | tf_op jit(solution)/shard_map/ppermute | solution.py:236
  154.2 3.9 %collective-permute-start.23 = (bf16[4,128,640]{2,1,0:T(8,128)(2,1)S(1)}, bf16[4,128,640]{2,1,0:T(8,128)(2,1)}, u32[]{:S(2)}, u32[]{:S(2)}) collective-permute-start(bf16[4,128,640]{2,1,0:T(8,128)(2,1)S(1)} %get-tuple-element.24), channel_id=1, source_target_pairs={{0,24},{1,25},{2,26},{3,27},{4,28},{5,29},{6,30},{7,31},{8,0},{9,1... | collective-permute-start | bytes 1966088 | tf_op jit(solution)/shard_map/ppermute | solution.py:236
  158.2 3.7 %collective-permute-start.3 = (f32[2,8,128]{2,1,0:T(8,128)S(1)}, f32[2,8,128]{2,1,0:T(8,128)S(1)}, u32[]{:S(2)}, u32[]{:S(2)}) collective-permute-start(f32[2,8,128]{2,1,0:T(8,128)S(1)} %pad_maximum_fusion.3), channel_id=1, source_target_pairs={{0,256},{32,288},{64,320},{96,352},{128,384},{160,416},{192,448},{... | collective-permute-start | bytes 24584 | tf_op jit(solution)/shard_map/ppermute | solution.py:208
  164.0 3.4 %collective-permute-start.24 = (bf16[2,128,640]{2,1,0:T(8,128)(2,1)S(1)}, bf16[2,128,640]{2,1,0:T(8,128)(2,1)S(1)}, u32[]{:S(2)}, u32[]{:S(2)}) collective-permute-start(bf16[2,128,640]{2,1,0:T(8,128)(2,1)S(1)} %picks.18), channel_id=1, source_target_pairs={{0,16},{1,17},{2,18},{3,19},{4,20},{5,21},{6,22},{7,23},{8,24},{9,... | collective-permute-start | bytes 983048 | tf_op jit(solution)/shard_map/ppermute | solution.py:236
  169.9 3.6 %collective-permute-start.25 = (bf16[2,128,640]{2,1,0:T(8,128)(2,1)S(1)}, bf16[2,128,640]{2,1,0:T(8,128)(2,1)S(1)}, u32[]{:S(2)}, u32[]{:S(2)}) collective-permute-start(bf16[2,128,640]{2,1,0:T(8,128)(2,1)S(1)} %get-tuple-element.25), channel_id=1, source_target_pairs={{0,8},{1,9},{2,10},{3,11},{4,12},{5,13},{6,14},{7,15},{8,16},{9,17... | collective-permute-start | bytes 983048 | tf_op jit(solution)/shard_map/ppermute | solution.py:236
  178.7 3.7 %collective-permute-done.24.refs_25_ = bf16[2,128,640]{2,1,0:T(8,128)(2,1)S(1)} collective-permute-done((bf16[2,128,640]{2,1,0:T(8,128)(2,1)S(1)}, bf16[2,128,640]{2,1,0:T(8,128)(2,1)S(1)}, u32[]{:S(2)}, u32[]{:S(2)}) %collective-permute-start.24) | collective-permute-done | bytes 327712 | tf_op jit(solution)/shard_map/ppermute | solution.py:236
  185.9 11.4 %grams.1 = (f32[8,64,8,128]{3,2,1,0:T(8,128)}, f32[8,64,8,128]{3,2,1,0:T(8,128)}) custom-call(s32[8,64]{1,0:T(8,128)S(1)} %bitcast.105, s32[4]{0:T(128)S(1)} %pad_add_fusion.refs_1_, s32[64,2]{1,0:T(8,128)S(1)} %copy.19.refs_2_, bf16[8,128,640]{2,1,0:T(8,128)(2,1)} %bitcast.106, bf16[8,128,640]{2,1,0:T(8,128)(2,1)} %pass_on.4.refs_2_.refs_4_, ...), custom_call_target="tpu_custom_call" | custom-call | flops 1342177280 | bytes 10485760 | tf_op jit(solution)/shard_map/grams/pallas_call | solution.py:174
  199.2 4.3 %collective-permute-done.27 = f32[8,64,8,128]{3,2,1,0:T(8,128)S(1)} collective-permute-done((f32[8,64,8,128]{3,2,1,0:T(8,128)}, f32[8,64,8,128]{3,2,1,0:T(8,128)S(1)}, u32[]{:S(2)}, u32[]{:S(2)}) %collective-permute-start.27) | collective-permute-done | bytes 2097184 | tf_op jit(solution)/shard_map/ppermute | solution.py:223
  205.4 34.1 %all_to_all.13 = f16[8,64,8,128]{3,2,1,0:T(8,128)(2,1)S(1)} all-to-all(f16[8,64,8,128]{3,2,1,0:T(8,128)(2,1)S(1)} %add_convert_fusion), channel_id=1, replica_groups={{0,64,128,192,256,320,384,448},{32,96,160,224,288,352,416,480},{1,65,12..., dimensions={0} | all-to-all | bytes 2097152 | tf_op jit(solution)/shard_map/all_to_all | solution.py:225
  (128 shorter events, 87.8 us)
Async XLA Ops:
  1.5 14.7 %all-to-all-start = ((s32[8,1,64]{2,1,0:T(1,128)}), s32[8,1,64]{2,1,0:T(1,128)S(1)}, u32[]{:S(2)}, u32[]{:S(2)}) async-start(s32[8,1,64]{2,1,0:T(1,128)} %broadcast_in_dim.9), calls=%async_computation | async-start | bytes 8192 | tf_op jit(solution)/shard_map/all_to_all | solution.py:238
  16.8 31.4 %collective-permute-start.8 = (bf16[8,128,640]{2,1,0:T(8,128)(2,1)}, bf16[8,128,640]{2,1,0:T(8,128)(2,1)}, u32[]{:S(2)}, u32[]{:S(2)}) collective-permute-start(bf16[8,128,640]{2,1,0:T(8,128)(2,1)} %pass_on.4.refs_2_.refs_4_), channel_id=1, source_target_pairs={{0,7},{1,0},{2,1},{3,2},{4,3},{5,4},{6,5},{7,6},{8,15},{9,8},{10,9... | collective-permute-start | bytes 3932168 | tf_op jit(solution)/shard_map/ppermute | solution.py:236
  19.4 33.3 %collective-permute-start.4 = (bf16[8,128,640]{2,1,0:T(8,128)(2,1)}, bf16[8,128,640]{2,1,0:T(8,128)(2,1)S(1)}, u32[]{:S(2)}, u32[]{:S(2)}) collective-permute-start(bf16[8,128,640]{2,1,0:T(8,128)(2,1)} %pass_on.4.refs_2_.refs_4_), channel_id=1, source_target_pairs={{0,1},{1,2},{2,3},{3,4},{4,5},{5,6},{6,7},{7,0},{8,9},{9,10},{10,1... | collective-permute-start | bytes 3932168 | tf_op jit(solution)/shard_map/ppermute | solution.py:236
  26.2 13.3 %collective-permute-start = (f32[2,8,128]{2,1,0:T(8,128)S(1)}, f32[2,8,128]{2,1,0:T(8,128)S(1)}, u32[]{:S(2)}, u32[]{:S(2)}) collective-permute-start(f32[2,8,128]{2,1,0:T(8,128)S(1)} %pad_maximum_fusion), channel_id=1, source_target_pairs={{0,32},{32,0},{64,96},{96,64},{128,160},{160,128},{192,224},{224,1... | collective-permute-start | bytes 24584 | tf_op jit(solution)/shard_map/ppermute | solution.py:208
  32.1 19.9 %collective-permute-start.5 = (bf16[2,128,640]{2,1,0:T(8,128)(2,1)S(1)}, bf16[2,128,640]{2,1,0:T(8,128)(2,1)S(1)}, u32[]{:S(2)}, u32[]{:S(2)}) collective-permute-start(bf16[2,128,640]{2,1,0:T(8,128)(2,1)S(1)} %picks.10), channel_id=1, source_target_pairs={{0,16},{1,17},{2,18},{3,19},{4,20},{5,21},{6,22},{7,23},{8,24},{9,... | collective-permute-start | bytes 983048 | tf_op jit(solution)/shard_map/ppermute | solution.py:236
  35.4 16.6 %collective-permute-start.6 = (bf16[2,128,640]{2,1,0:T(8,128)(2,1)S(1)}, bf16[2,128,640]{2,1,0:T(8,128)(2,1)S(1)}, u32[]{:S(2)}, u32[]{:S(2)}) collective-permute-start(bf16[2,128,640]{2,1,0:T(8,128)(2,1)S(1)} %get-tuple-element.17), channel_id=1, source_target_pairs={{0,8},{1,9},{2,10},{3,11},{4,12},{5,13},{6,14},{7,15},{8,16},{9,17... | collective-permute-start | bytes 983048 | tf_op jit(solution)/shard_map/ppermute | solution.py:236
  39.5 13.2 %collective-permute-start.7 = (bf16[2,128,640]{2,1,0:T(8,128)(2,1)S(1)}, bf16[2,128,640]{2,1,0:T(8,128)(2,1)S(1)}, u32[]{:S(2)}, u32[]{:S(2)}) collective-permute-start(bf16[2,128,640]{2,1,0:T(8,128)(2,1)S(1)} %get-tuple-element.18), channel_id=1, source_target_pairs={{0,24},{1,25},{2,26},{3,27},{4,28},{5,29},{6,30},{7,31},{8,0},{9,1... | collective-permute-start | bytes 983048 | tf_op jit(solution)/shard_map/ppermute | solution.py:236
  48.2 30.4 %collective-permute-start.12 = (bf16[8,128,640]{2,1,0:T(8,128)(2,1)}, bf16[8,128,640]{2,1,0:T(8,128)(2,1)}, u32[]{:S(2)}, u32[]{:S(2)}) collective-permute-start(bf16[8,128,640]{2,1,0:T(8,128)(2,1)} %collective-permute-done.8.refs_3_.refs_6_), channel_id=1, source_target_pairs={{0,7},{1,0},{2,1},{3,2},{4,3},{5,4},{6,5},{7,6},{8,15},{9,8},{10,9... | collective-permute-start | bytes 3932168 | tf_op jit(solution)/shard_map/ppermute | solution.py:236
  54.4 33.6 %collective-permute-start.9 = (bf16[8,128,640]{2,1,0:T(8,128)(2,1)}, bf16[8,128,640]{2,1,0:T(8,128)(2,1)S(1)}, u32[]{:S(2)}, u32[]{:S(2)}) collective-permute-start(bf16[8,128,640]{2,1,0:T(8,128)(2,1)} %pass_on.5.refs_2_.refs_5_), channel_id=1, source_target_pairs={{0,1},{1,2},{2,3},{3,4},{4,5},{5,6},{6,7},{7,0},{8,9},{9,10},{10,1... | collective-permute-start | bytes 3932168 | tf_op jit(solution)/shard_map/ppermute | solution.py:236
  61.6 25.5 %collective-permute-start.10 = (bf16[4,128,640]{2,1,0:T(8,128)(2,1)S(1)}, bf16[4,128,640]{2,1,0:T(8,128)(2,1)S(1)}, u32[]{:S(2)}, u32[]{:S(2)}) collective-permute-start(bf16[4,128,640]{2,1,0:T(8,128)(2,1)S(1)} %get-tuple-element.19), channel_id=1, source_target_pairs={{0,8},{1,9},{2,10},{3,11},{4,12},{5,13},{6,14},{7,15},{8,16},{9,17... | collective-permute-start | bytes 1966088 | tf_op jit(solution)/shard_map/ppermute | solution.py:236
  65.6 21.5 %collective-permute-start.11 = (bf16[4,128,640]{2,1,0:T(8,128)(2,1)S(1)}, bf16[4,128,640]{2,1,0:T(8,128)(2,1)}, u32[]{:S(2)}, u32[]{:S(2)}) collective-permute-start(bf16[4,128,640]{2,1,0:T(8,128)(2,1)S(1)} %get-tuple-element.20), channel_id=1, source_target_pairs={{0,24},{1,25},{2,26},{3,27},{4,28},{5,29},{6,30},{7,31},{8,0},{9,1... | collective-permute-start | bytes 1966088 | tf_op jit(solution)/shard_map/ppermute | solution.py:236
  78.5 45.8 %collective-permute-start.16 = (bf16[8,128,640]{2,1,0:T(8,128)(2,1)}, bf16[8,128,640]{2,1,0:T(8,128)(2,1)S(1)}, u32[]{:S(2)}, u32[]{:S(2)}) collective-permute-start(bf16[8,128,640]{2,1,0:T(8,128)(2,1)} %collective-permute-done.12.refs_3_.refs_8_), channel_id=1, source_target_pairs={{0,7},{1,0},{2,1},{3,2},{4,3},{5,4},{6,5},{7,6},{8,15},{9,8},{10,9... | collective-permute-start | bytes 3932168 | tf_op jit(solution)/shard_map/ppermute | solution.py:236
  83.8 25.6 %collective-permute-start.14 = (bf16[4,128,640]{2,1,0:T(8,128)(2,1)}, bf16[4,128,640]{2,1,0:T(8,128)(2,1)}, u32[]{:S(2)}, u32[]{:S(2)}) collective-permute-start(bf16[4,128,640]{2,1,0:T(8,128)(2,1)} %picks.13), channel_id=1, source_target_pairs={{0,16},{1,17},{2,18},{3,19},{4,20},{5,21},{6,22},{7,23},{8,24},{9,... | collective-permute-start | bytes 1966088 | tf_op jit(solution)/shard_map/ppermute | solution.py:236
  89.1 45.7 %collective-permute-start.13 = (bf16[8,128,640]{2,1,0:T(8,128)(2,1)}, bf16[8,128,640]{2,1,0:T(8,128)(2,1)S(1)}, u32[]{:S(2)}, u32[]{:S(2)}) collective-permute-start(bf16[8,128,640]{2,1,0:T(8,128)(2,1)} %pass_on.6.refs_2_.refs_7_), channel_id=1, source_target_pairs={{0,1},{1,2},{2,3},{3,4},{4,5},{5,6},{6,7},{7,0},{8,9},{9,10},{10,1... | collective-permute-start | bytes 3932168 | tf_op jit(solution)/shard_map/ppermute | solution.py:236
  113.1 19.7 %collective-permute-start.15 = (bf16[4,128,640]{2,1,0:T(8,128)(2,1)S(1)}, bf16[4,128,640]{2,1,0:T(8,128)(2,1)S(1)}, u32[]{:S(2)}, u32[]{:S(2)}) collective-permute-start(bf16[4,128,640]{2,1,0:T(8,128)(2,1)S(1)} %picks.14), channel_id=1, source_target_pairs={{0,16},{1,17},{2,18},{3,19},{4,20},{5,21},{6,22},{7,23},{8,24},{9,... | collective-permute-start | bytes 1966088 | tf_op jit(solution)/shard_map/ppermute | solution.py:236
  118.5 29.0 %collective-permute-start.19 = (bf16[4,128,640]{2,1,0:T(8,128)(2,1)}, bf16[4,128,640]{2,1,0:T(8,128)(2,1)}, u32[]{:S(2)}, u32[]{:S(2)}) collective-permute-start(bf16[4,128,640]{2,1,0:T(8,128)(2,1)} %get-tuple-element.21), channel_id=1, source_target_pairs={{0,8},{1,9},{2,10},{3,11},{4,12},{5,13},{6,14},{7,15},{8,16},{9,17... | collective-permute-start | bytes 1966088 | tf_op jit(solution)/shard_map/ppermute | solution.py:236
  120.4 28.6 %collective-permute-start.20 = (bf16[4,128,640]{2,1,0:T(8,128)(2,1)}, bf16[4,128,640]{2,1,0:T(8,128)(2,1)}, u32[]{:S(2)}, u32[]{:S(2)}) collective-permute-start(bf16[4,128,640]{2,1,0:T(8,128)(2,1)} %get-tuple-element.22), channel_id=1, source_target_pairs={{0,24},{1,25},{2,26},{3,27},{4,28},{5,29},{6,30},{7,31},{8,0},{9,1... | collective-permute-start | bytes 1966088 | tf_op jit(solution)/shard_map/ppermute | solution.py:236
  125.4 32.8 %collective-permute-start.18 = (bf16[8,64,640]{2,1,0:T(8,128)(2,1)}, bf16[8,64,640]{2,1,0:T(8,128)(2,1)}, u32[]{:S(2)}, u32[]{:S(2)}) collective-permute-start(bf16[8,64,640]{2,1,0:T(8,128)(2,1)} %slice.53), channel_id=1, source_target_pairs={{0,7},{1,0},{2,1},{3,2},{4,3},{5,4},{6,5},{7,6},{8,15},{9,8},{10,9... | collective-permute-start | bytes 1966088 | tf_op jit(solution)/shard_map/ppermute | solution.py:236
  137.9 24.1 %collective-permute-start.17 = (bf16[8,64,640]{2,1,0:T(8,128)(2,1)}, bf16[8,64,640]{2,1,0:T(8,128)(2,1)S(1)}, u32[]{:S(2)}, u32[]{:S(2)}) collective-permute-start(bf16[8,64,640]{2,1,0:T(8,128)(2,1)} %slice.52), channel_id=1, source_target_pairs={{0,1},{1,2},{2,3},{3,4},{4,5},{5,6},{6,7},{7,0},{8,9},{9,10},{10,1... | collective-permute-start | bytes 1966088 | tf_op jit(solution)/shard_map/ppermute | solution.py:236
  145.3 28.3 %collective-permute-start.21 = (bf16[4,128,640]{2,1,0:T(8,128)(2,1)S(1)}, bf16[4,128,640]{2,1,0:T(8,128)(2,1)}, u32[]{:S(2)}, u32[]{:S(2)}) collective-permute-start(bf16[4,128,640]{2,1,0:T(8,128)(2,1)S(1)} %picks.16), channel_id=1, source_target_pairs={{0,16},{1,17},{2,18},{3,19},{4,20},{5,21},{6,22},{7,23},{8,24},{9,... | collective-permute-start | bytes 1966088 | tf_op jit(solution)/shard_map/ppermute | solution.py:236
  152.3 25.6 %collective-permute-start.22 = (bf16[4,128,640]{2,1,0:T(8,128)(2,1)}, bf16[4,128,640]{2,1,0:T(8,128)(2,1)S(1)}, u32[]{:S(2)}, u32[]{:S(2)}) collective-permute-start(bf16[4,128,640]{2,1,0:T(8,128)(2,1)} %get-tuple-element.23), channel_id=1, source_target_pairs={{0,8},{1,9},{2,10},{3,11},{4,12},{5,13},{6,14},{7,15},{8,16},{9,17... | collective-permute-start | bytes 1966088 | tf_op jit(solution)/shard_map/ppermute | solution.py:236
  154.2 24.5 %collective-permute-start.23 = (bf16[4,128,640]{2,1,0:T(8,128)(2,1)S(1)}, bf16[4,128,640]{2,1,0:T(8,128)(2,1)}, u32[]{:S(2)}, u32[]{:S(2)}) collective-permute-start(bf16[4,128,640]{2,1,0:T(8,128)(2,1)S(1)} %get-tuple-element.24), channel_id=1, source_target_pairs={{0,24},{1,25},{2,26},{3,27},{4,28},{5,29},{6,30},{7,31},{8,0},{9,1... | collective-permute-start | bytes 1966088 | tf_op jit(solution)/shard_map/ppermute | solution.py:236
  164.0 18.4 %collective-permute-start.24 = (bf16[2,128,640]{2,1,0:T(8,128)(2,1)S(1)}, bf16[2,128,640]{2,1,0:T(8,128)(2,1)S(1)}, u32[]{:S(2)}, u32[]{:S(2)}) collective-permute-start(bf16[2,128,640]{2,1,0:T(8,128)(2,1)S(1)} %picks.18), channel_id=1, source_target_pairs={{0,16},{1,17},{2,18},{3,19},{4,20},{5,21},{6,22},{7,23},{8,24},{9,... | collective-permute-start | bytes 983048 | tf_op jit(solution)/shard_map/ppermute | solution.py:236
  169.9 13.5 %collective-permute-start.25 = (bf16[2,128,640]{2,1,0:T(8,128)(2,1)S(1)}, bf16[2,128,640]{2,1,0:T(8,128)(2,1)S(1)}, u32[]{:S(2)}, u32[]{:S(2)}) collective-permute-start(bf16[2,128,640]{2,1,0:T(8,128)(2,1)S(1)} %get-tuple-element.25), channel_id=1, source_target_pairs={{0,8},{1,9},{2,10},{3,11},{4,12},{5,13},{6,14},{7,15},{8,16},{9,17... | collective-permute-start | bytes 983048 | tf_op jit(solution)/shard_map/ppermute | solution.py:236
  (32 other events, 253.7 us)
